TPU v7x, 256 devices: a whole 4x4x8 slice. The times are simulated.
256 devices in a mesh: hist: 4 (over y), ent: 64 (over x, z, core).
Axes of the slice: x: 4, y: 4, z: 8, core: 2. Of those that a mesh axis runs over, the one named last changes fastest.
Arguments:
- states: bfloat16 [4, 16384, 512], P('hist', 'ent'), may hold values from -6 to 6
- w_neigh: bfloat16 [2, 256, 256], replicated, may hold values from -0.375 to 0.375
- w_self: bfloat16 [512, 512], replicated, may hold values from -0.25 to 0.25
- w_gate: bfloat16 [512, 512], replicated, may hold values from -0.25 to 0.25
- b_gate: float32 [512], replicated, may hold values from -4 to 4
- relation: bfloat16 [460, 512], replicated, may hold values from -6 to 6
- edge_src: int32 [4, 32768], P('hist', 'ent'), may hold values from 0 to 255
- edge_rel: int32 [4, 32768], P('hist', 'ent'), may hold values from 0 to 459
- edge_dst: int32 [4, 32768], P('hist', 'ent'), may hold values from 0 to 255
- send_counts: int32 [4, 4096], P('hist', 'ent'), may hold values from 1 to 8, as said below
- query_ent: int32 [8192], P('ent'), may hold values from 0 to 255
- query_rel: int32 [8192], P('ent'), may hold values from 0 to 459
- query_grad: float32 [8192, 512], P('ent'), may hold values from -6 to 6
Outputs:
- grad_states: float32 [4, 16384, 512], P('hist', 'ent')
- grad_neigh: float32 [2, 256, 256], replicated
- grad_self: float32 [512, 512], replicated
- grad_gate: float32 [512, 512], replicated
- grad_bias: float32 [512], replicated
- grad_relation: float32 [460, 512], replicated
Inputs may be any that keep to these rules, and one draw needn't show every extreme that they name: `send_counts`: slots at or beyond their bucket's count hold arbitrary ids and carry no edge. In every snapshot one target partition receives exactly 8 slots in use from every source partition; which one is drawn.
All inputs are finite; a program needn't handle non-finite values.
Results may differ from a plain program's by a relative error of at most 0.0053.
Values may be sent and summed in bfloat16 or wider, within the bound.
A program may use at most 64 MiB of HBM per device.

v0:
```python
import math

import jax
import jax.numpy as jnp
from jax import lax
from jax.sharding import PartitionSpec as P


def from_behind(block, axis, distance):
    devices = range(lax.axis_size(axis))
    route = [(i - distance, i) for i in devices if i - distance in devices]
    return lax.ppermute(block, axis, route)


def on_device(
    states,
    w_neigh,
    w_self,
    w_gate,
    b_gate,
    relation,
    edge_src,
    edge_rel,
    edge_dst,
    send_counts,
    query_ent,
    query_rel,
    query_grad,
):
    groups = lax.axis_size("ent")
    sections = lax.axis_size("hist")
    position = lax.axis_index("hist")
    ent_rows = states.shape[1]
    features = states.shape[2]
    blocks = w_neigh.shape[0]
    block_width = w_neigh.shape[1]
    edges_here = edge_src.shape[1]
    bucket_slots = edges_here // groups
    hidden = states[0]
    src_ids = edge_src[0]
    rel_ids = edge_rel[0]
    within = lax.broadcasted_iota(jnp.int32, (groups, bucket_slots), 1)
    in_use = within < send_counts[0][:, None]
    targets = jnp.where(in_use, edge_dst[0].reshape(groups, bucket_slots), -1)
    arrived = lax.all_to_all(targets, "ent", split_axis=0, concat_axis=0, tiled=True).reshape(
        edges_here
    )
    arrived_live = (arrived >= 0).astype(jnp.float32)
    landing = jnp.maximum(arrived, 0)
    live_flat = in_use.reshape(edges_here).astype(jnp.float32)
    indegree = jnp.zeros((ent_rows,), jnp.float32).at[landing].add(arrived_live)
    scaling = 1.0 / jnp.maximum(indegree, 1.0)
    inputs = (hidden[src_ids].astype(jnp.float32) + relation[rel_ids].astype(jnp.float32)).astype(
        jnp.bfloat16
    )
    product = jnp.einsum(
        "ebi,bij->ebj",
        inputs.reshape(edges_here, blocks, block_width),
        w_neigh,
        preferred_element_type=jnp.float32,
    )
    message = (product.reshape(edges_here, features) * live_flat[:, None]).astype(jnp.bfloat16)
    received = lax.all_to_all(
        message.reshape(groups, bucket_slots, features),
        "ent",
        split_axis=0,
        concat_axis=0,
        tiled=True,
    )
    summed = (
        jnp.zeros((ent_rows, features), jnp.float32)
        .at[landing]
        .add(received.reshape(edges_here, features).astype(jnp.float32))
    )
    pre_act = summed * scaling[:, None] + jnp.dot(
        hidden, w_self, preferred_element_type=jnp.float32
    )
    gate_open = jax.nn.sigmoid(jnp.dot(hidden, w_gate, preferred_element_type=jnp.float32) + b_gate)
    sigmoid_pre = jax.nn.sigmoid(pre_act)
    new_state = pre_act * sigmoid_pre
    contract = (((0,), (0,)), ((), ()))
    onehot = (query_ent[:, None] == lax.broadcasted_iota(jnp.int32, (1, ent_rows), 1)).astype(
        jnp.float32
    )
    top_grad = lax.dot_general(
        onehot,
        query_grad,
        contract,
        precision=lax.Precision.HIGHEST,
        preferred_element_type=jnp.float32,
    )
    query_part = jax.ops.segment_sum(query_grad, query_rel, num_segments=relation.shape[0])
    cotangent = top_grad
    totals = None
    result = jnp.zeros((ent_rows, features), jnp.float32)
    for step_index in range(sections):
        active = position == sections - 1 - step_index
        keep_part = cotangent * (1.0 - gate_open)
        gate_term = (
            cotangent * (new_state - hidden.astype(jnp.float32)) * gate_open * (1.0 - gate_open)
        )
        backward_gate_low = gate_term.astype(jnp.bfloat16)
        pre_term = cotangent * gate_open * (sigmoid_pre * (1.0 + pre_act * (1.0 - sigmoid_pre)))
        backward_pre_low = pre_term.astype(jnp.bfloat16)
        backward_grad_bias = jnp.sum(gate_term, axis=0)
        back_sum = keep_part + jnp.dot(
            backward_gate_low, w_gate.T, preferred_element_type=jnp.float32
        )
        back_sum = back_sum + jnp.dot(
            backward_pre_low, w_self.T, preferred_element_type=jnp.float32
        )
        replies = (pre_term[landing] * scaling[landing][:, None] * arrived_live[:, None]).astype(
            jnp.bfloat16
        )
        backward_returned = lax.all_to_all(
            replies.reshape(groups, bucket_slots, features),
            "ent",
            split_axis=0,
            concat_axis=0,
            tiled=True,
        )
        backward_returned = backward_returned.reshape(edges_here, blocks, block_width)
        backward_spread = jnp.einsum(
            "ebj,bij->ebi", backward_returned, w_neigh, preferred_element_type=jnp.float32
        ).reshape(edges_here, features)
        back_sum = back_sum + jnp.zeros((ent_rows, features), jnp.float32).at[src_ids].add(
            backward_spread
        )
        back_sum, pieces = (
            back_sum,
            (
                backward_gate_low,
                backward_pre_low,
                backward_grad_bias,
                backward_returned,
                backward_spread,
            ),
        )
        gate_low, pre_low, contract_grad_bias, returned, spread = pieces
        contract_grad_gate = lax.dot_general(
            hidden, gate_low, contract, preferred_element_type=jnp.float32
        )
        contract_grad_self = lax.dot_general(
            hidden, pre_low, contract, preferred_element_type=jnp.float32
        )
        contract_grad_neigh = jnp.einsum(
            "ebi,ebj->bij",
            inputs.reshape(edges_here, blocks, block_width),
            returned,
            preferred_element_type=jnp.float32,
        )
        contract_grad_rel = jax.ops.segment_sum(spread, rel_ids, num_segments=relation.shape[0])
        grads = (
            contract_grad_neigh,
            contract_grad_self,
            contract_grad_gate,
            contract_grad_bias,
            contract_grad_rel,
        )
        masked = tuple((jnp.where(active, item, jnp.zeros_like(item)) for item in grads))
        if totals is None:
            totals = masked
        else:
            totals = tuple((a + b for a, b in zip(totals, masked)))
        result = jnp.where(active, back_sum, result)
        if step_index + 1 < sections:
            cotangent = from_behind(back_sum, "hist", -1)
    grad_neigh, grad_self, grad_gate, grad_bias, grad_rel = totals
    grad_rel = grad_rel + jnp.where(
        position == sections - 1, query_part, jnp.zeros_like(query_part)
    )
    grad_neigh, grad_self, grad_gate, grad_bias, grad_rel = lax.psum(
        (grad_neigh, grad_self, grad_gate, grad_bias, grad_rel), ("hist", "ent")
    )
    factor = 1.0 / math.sqrt(sections * ent_rows * groups)
    return (
        result[None],
        grad_neigh * factor,
        grad_self * factor,
        grad_gate * factor,
        grad_bias * factor,
        grad_rel * factor,
    )


def solution(mesh):
    return jax.shard_map(
        on_device,
        mesh=mesh,
        in_specs=(
            P("hist", "ent", None),
            P(),
            P(),
            P(),
            P(),
            P(),
            P("hist", "ent"),
            P("hist", "ent"),
            P("hist", "ent"),
            P("hist", "ent"),
            P("ent"),
            P("ent"),
            P("ent", None),
        ),
        out_specs=(P("hist", "ent", None), P(), P(), P(), P(), P()),
        check_vma=False,
    )
```

profile of v0, /device:TPU:1, one launch (start us, length us, event | category | flops | bytes accessed | tf_op | source)
XLA Modules:
  0.0 562.2 jit_solution(392604421657310684)
XLA Ops:
  10.5 13.0 %all-to-all-start = ((s32[64,1,8]{2,1,0:T(1,128)}), s32[64,1,8]{2,1,0:T(1,128)S(1)}, u32[]{:S(2)}, u32[]{:S(2)}) async-start(s32[64,1,8]{2,1,0:T(1,128)} %bitcast.2), calls=%async_computation | async-start | bytes 65536 | tf_op jit(solution)/shard_map/all_to_all | solution.py:45
  36.1 10.5 %all-to-all-start.1 = ((bf16[64,8,512]{2,1,0:T(8,128)(2,1)}), bf16[64,8,512]{2,1,0:T(8,128)(2,1)S(1)}, u32[]{:S(2)}, u32[]{:S(2)}) async-start(bf16[64,8,512]{2,1,0:T(8,128)(2,1)} %multiply_convert_fusion), calls=%async_computation.1 | async-start | bytes 1048576 | tf_op jit(solution)/shard_map/all_to_all | solution.py:63
  56.1 7.8 %all-to-all-done.1 = bf16[64,8,512]{2,1,0:T(8,128)(2,1)S(1)} async-done(((bf16[64,8,512]{2,1,0:T(8,128)(2,1)}), bf16[64,8,512]{2,1,0:T(8,128)(2,1)S(1)}, u32[]{:S(2)}, u32[]{:S(2)}) %all-to-all-start.1) | async-done | bytes 524320 | tf_op jit(solution)/shard_map/all_to_all | solution.py:63
  74.2 6.5 %all-to-all-start.2 = ((bf16[64,8,512]{2,1,0:T(8,128)(2,1)}), bf16[64,8,512]{2,1,0:T(8,128)(2,1)}, u32[]{:S(2)}, u32[]{:S(2)}) async-start(bf16[64,8,512]{2,1,0:T(8,128)(2,1)} %fusion.24), calls=%async_computation.2 | async-start | bytes 1048576 | tf_op jit(solution)/shard_map/all_to_all | solution.py:115
  82.7 15.1 %all-to-all-done.2 = bf16[64,8,512]{2,1,0:T(8,128)(2,1)} async-done(((bf16[64,8,512]{2,1,0:T(8,128)(2,1)}), bf16[64,8,512]{2,1,0:T(8,128)(2,1)}, u32[]{:S(2)}, u32[]{:S(2)}) %all-to-all-start.2) | async-done | bytes 524320 | tf_op jit(solution)/shard_map/all_to_all | solution.py:115
  102.9 4.5 scatter_fusion
  108.7 13.8 %collective-permute-done = f32[256,512]{1,0:T(8,128)S(1)} collective-permute-done((f32[256,512]{1,0:T(8,128)S(1)}, f32[256,512]{1,0:T(8,128)S(1)}, u32[]{:S(2)}, u32[]{:S(2)}) %collective-permute-start) | collective-permute-done | bytes 524320 | tf_op jit(solution)/shard_map/ppermute | solution.py:12
  128.1 6.9 %all-to-all-start.3 = ((bf16[64,8,512]{2,1,0:T(8,128)(2,1)}), bf16[64,8,512]{2,1,0:T(8,128)(2,1)}, u32[]{:S(2)}, u32[]{:S(2)}) async-start(bf16[64,8,512]{2,1,0:T(8,128)(2,1)} %fusion.22), calls=%async_computation.3 | async-start | bytes 1048576 | tf_op jit(solution)/shard_map/all_to_all | solution.py:115
  141.9 10.4 %all-to-all-done.3 = bf16[64,8,512]{2,1,0:T(8,128)(2,1)} async-done(((bf16[64,8,512]{2,1,0:T(8,128)(2,1)}), bf16[64,8,512]{2,1,0:T(8,128)(2,1)}, u32[]{:S(2)}, u32[]{:S(2)}) %all-to-all-start.3) | async-done | bytes 524320 | tf_op jit(solution)/shard_map/all_to_all | solution.py:115
  159.3 4.7 scatter_fusion.1
  166.6 5.2 scatter_custom_fusion.6
  174.4 4.8 collective-permute-done.1
  185.8 7.1 %all-to-all-start.4 = ((bf16[64,8,512]{2,1,0:T(8,128)(2,1)}), bf16[64,8,512]{2,1,0:T(8,128)(2,1)}, u32[]{:S(2)}, u32[]{:S(2)}) async-start(bf16[64,8,512]{2,1,0:T(8,128)(2,1)} %fusion.20), calls=%async_computation.4 | async-start | bytes 1048576 | tf_op jit(solution)/shard_map/all_to_all | solution.py:115
  195.5 5.6 scatter_custom_fusion.7
  205.8 4.4 all-to-all-done.4
  217.0 4.5 scatter_fusion.2
  227.0 5.2 scatter_custom_fusion.8
  232.2 4.7 collective-permute-done.2
  243.7 7.1 %all-to-all-start.5 = ((bf16[64,8,512]{2,1,0:T(8,128)(2,1)}), bf16[64,8,512]{2,1,0:T(8,128)(2,1)}, u32[]{:S(2)}, u32[]{:S(2)}) async-start(bf16[64,8,512]{2,1,0:T(8,128)(2,1)} %fusion.18), calls=%async_computation.5 | async-start | bytes 1048576 | tf_op jit(solution)/shard_map/all_to_all | solution.py:115
  256.5 11.5 %all-to-all-done.5 = bf16[64,8,512]{2,1,0:T(8,128)(2,1)} async-done(((bf16[64,8,512]{2,1,0:T(8,128)(2,1)}), bf16[64,8,512]{2,1,0:T(8,128)(2,1)}, u32[]{:S(2)}, u32[]{:S(2)}) %all-to-all-start.5) | async-done | bytes 524320 | tf_op jit(solution)/shard_map/all_to_all | solution.py:115
  276.0 5.2 scatter_custom_fusion.9
  284.0 75.1 %psum.38 = f32[512]{0:T(512)S(1)} all-reduce(f32[512]{0:T(512)S(1)} %select_add_fusion.1), channel_id=1, replica_groups=mesh['hist'=4,'ent'=64] {'hist','ent'}, use_global_device_ids=true, to_apply=%region_13.14 | all-reduce | flops 512 | bytes 4096 | tf_op jit(solution)/shard_map/psum | solution.py:172
  362.3 4.5 scatter_fusion.3
  367.8 180.3 %all-reduce.3.cloned.1.call-done = (f32[2,256,256]{2,1,0:T(8,128)}, f32[512,512]{0,1:T(8,128)}, f32[512,512]{0,1:T(8,128)}, f32[460,512]{1,0:T(8,128)}) async-done(((f32[2,256,256]{2,1,0:T(8,128)}, f32[512,512]{0,1:T(8,128)}, f32[512,512]{0,1:T(8,128)}, f32[460,512]{1,0:T(8,128)}), (f32[2,256,256]{2,1,0:T(8,128)}, f32[512,512]{0,1:T(8,128)}, f32[512,512]{0,1:T(8,128)}, ...) | async-done | bytes 3563536 | tf_op jit(solution)/shard_map/psum | solution.py:172
  (172 shorter events, 129.0 us)
Async XLA Ops:
  7.2 61.1 %copy-start = (bf16[512,512]{1,0:T(8,128)(2,1)S(1)}, bf16[512,512]{1,0:T(8,128)(2,1)}, u32[]{:S(2)}) copy-start(bf16[512,512]{1,0:T(8,128)(2,1)} %param.16) | copy-start | bytes 1572868
  10.5 25.7 %all-to-all-start = ((s32[64,1,8]{2,1,0:T(1,128)}), s32[64,1,8]{2,1,0:T(1,128)S(1)}, u32[]{:S(2)}, u32[]{:S(2)}) async-start(s32[64,1,8]{2,1,0:T(1,128)} %bitcast.2), calls=%async_computation | async-start | bytes 65536 | tf_op jit(solution)/shard_map/all_to_all | solution.py:45
  36.1 10.5 %copy-start.35 = (f32[128,512]{1,0:T(8,128)S(1)}, f32[128,512]{1,0:T(8,128)}, u32[]{:S(2)}) copy-start(f32[128,512]{1,0:T(8,128)} %param.25) | copy-start | bytes 786436
  36.1 10.5 %copy-start.39 = (s32[128]{0:T(128)S(1)}, s32[128]{0:T(128)}, u32[]{:S(2)}) copy-start(s32[128]{0:T(128)} %param.23) | copy-start | bytes 1540
  36.1 27.8 %all-to-all-start.1 = ((bf16[64,8,512]{2,1,0:T(8,128)(2,1)}), bf16[64,8,512]{2,1,0:T(8,128)(2,1)S(1)}, u32[]{:S(2)}, u32[]{:S(2)}) async-start(bf16[64,8,512]{2,1,0:T(8,128)(2,1)} %multiply_convert_fusion), calls=%async_computation.1 | async-start | bytes 1048576 | tf_op jit(solution)/shard_map/all_to_all | solution.py:63
  56.1 11.8 %copy-start.1 = (bf16[1,256,512]{2,1,0:T(8,128)(2,1)S(1)}, bf16[1,256,512]{2,1,0:T(8,128)(2,1)}, u32[]{:S(2)}) copy-start(bf16[1,256,512]{2,1,0:T(8,128)(2,1)} %param.13) | copy-start | bytes 786436
  56.1 11.8 %copy-start.5 = (bf16[512,512]{1,0:T(8,128)(2,1)S(1)}, bf16[512,512]{1,0:T(8,128)(2,1)}, u32[]{:S(2)}) copy-start(bf16[512,512]{1,0:T(8,128)(2,1)} %param.15) | copy-start | bytes 1572868
  69.0 11.7 %copy-start.12 = (f32[256,512]{1,0:T(8,128)}, f32[256,512]{1,0:T(8,128)S(1)}, u32[]{:S(2)}) copy-start(f32[256,512]{1,0:T(8,128)S(1)} %convolution_add_fusion.2) | copy-start | bytes 1572868
  69.6 167.2 %copy-start.3 = (f32[256,512]{1,0:T(8,128)}, f32[256,512]{1,0:T(8,128)S(1)}, u32[]{:S(2)}) copy-start(f32[256,512]{1,0:T(8,128)S(1)} %get-tuple-element.39) | copy-start | bytes 1572868
  74.2 23.7 %all-to-all-start.2 = ((bf16[64,8,512]{2,1,0:T(8,128)(2,1)}), bf16[64,8,512]{2,1,0:T(8,128)(2,1)}, u32[]{:S(2)}, u32[]{:S(2)}) async-start(bf16[64,8,512]{2,1,0:T(8,128)(2,1)} %fusion.24), calls=%async_computation.2 | async-start | bytes 1048576 | tf_op jit(solution)/shard_map/all_to_all | solution.py:115
  102.9 19.6 %copy-start.13 = (f32[256,512]{1,0:T(8,128)S(1)}, f32[256,512]{1,0:T(8,128)}, u32[]{:S(2)}) copy-start(f32[256,512]{1,0:T(8,128)} %copy-done.12) | copy-start | bytes 1572868
  107.4 15.1 %collective-permute-start = (f32[256,512]{1,0:T(8,128)S(1)}, f32[256,512]{1,0:T(8,128)S(1)}, u32[]{:S(2)}, u32[]{:S(2)}) collective-permute-start(f32[256,512]{1,0:T(8,128)S(1)} %scatter_fusion), channel_id=1, source_target_pairs={{64,0},{128,64},{192,128},{65,1},{129,65},{193,129},{66,2},{130,66... | collective-permute-start | bytes 1572872 | tf_op jit(solution)/shard_map/ppermute | solution.py:12
  128.1 24.2 %all-to-all-start.3 = ((bf16[64,8,512]{2,1,0:T(8,128)(2,1)}), bf16[64,8,512]{2,1,0:T(8,128)(2,1)}, u32[]{:S(2)}, u32[]{:S(2)}) async-start(bf16[64,8,512]{2,1,0:T(8,128)(2,1)} %fusion.22), calls=%async_computation.3 | async-start | bytes 1048576 | tf_op jit(solution)/shard_map/all_to_all | solution.py:115
  164.0 15.2 %collective-permute-start.1 = (f32[256,512]{1,0:T(8,128)S(1)}, f32[256,512]{1,0:T(8,128)}, u32[]{:S(2)}, u32[]{:S(2)}) collective-permute-start(f32[256,512]{1,0:T(8,128)S(1)} %scatter_fusion.1), channel_id=1, source_target_pairs={{64,0},{128,64},{192,128},{65,1},{129,65},{193,129},{66,2},{130,66... | collective-permute-start | bytes 1572872 | tf_op jit(solution)/shard_map/ppermute | solution.py:12
  171.8 7.4 %copy-start.14 = (f32[256,512]{1,0:T(8,128)S(1)}, f32[256,512]{1,0:T(8,128)}, u32[]{:S(2)}) copy-start(f32[256,512]{1,0:T(8,128)} %copy-done.12) | copy-start | bytes 1572868
  185.8 7.1 %copy-start.24 = (bf16[256,512]{1,0:T(8,128)(2,1)S(1)}, bf16[256,512]{1,0:T(8,128)(2,1)}, u32[]{:S(2)}) copy-start(bf16[256,512]{1,0:T(8,128)(2,1)} %get-tuple-element.29) | copy-start | bytes 786436
  185.8 24.3 %all-to-all-start.4 = ((bf16[64,8,512]{2,1,0:T(8,128)(2,1)}), bf16[64,8,512]{2,1,0:T(8,128)(2,1)}, u32[]{:S(2)}, u32[]{:S(2)}) async-start(bf16[64,8,512]{2,1,0:T(8,128)(2,1)} %fusion.20), calls=%async_computation.4 | async-start | bytes 1048576 | tf_op jit(solution)/shard_map/all_to_all | solution.py:115
  195.5 5.6 %copy-start.10 = (bf16[512,512]{0,1:T(8,128)(2,1)S(1)}, bf16[512,512]{0,1:T(8,128)(2,1)}, u32[]{:S(2)}) copy-start(bf16[512,512]{0,1:T(8,128)(2,1)} %copy-done.9) | copy-start | bytes 1572868
  221.5 15.3 %collective-permute-start.2 = (f32[256,512]{1,0:T(8,128)S(1)}, f32[256,512]{1,0:T(8,128)}, u32[]{:S(2)}, u32[]{:S(2)}) collective-permute-start(f32[256,512]{1,0:T(8,128)S(1)} %scatter_fusion.2), channel_id=1, source_target_pairs={{64,0},{128,64},{192,128},{65,1},{129,65},{193,129},{66,2},{130,66... | collective-permute-start | bytes 1572872 | tf_op jit(solution)/shard_map/ppermute | solution.py:12
  243.7 7.3 %copy-start.11 = (bf16[512,512]{0,1:T(8,128)(2,1)S(1)}, bf16[512,512]{0,1:T(8,128)(2,1)}, u32[]{:S(2)}) copy-start(bf16[512,512]{0,1:T(8,128)(2,1)} %copy-done.9) | copy-start | bytes 1572868
  243.7 24.3 %all-to-all-start.5 = ((bf16[64,8,512]{2,1,0:T(8,128)(2,1)}), bf16[64,8,512]{2,1,0:T(8,128)(2,1)}, u32[]{:S(2)}, u32[]{:S(2)}) async-start(bf16[64,8,512]{2,1,0:T(8,128)(2,1)} %fusion.18), calls=%async_computation.5 | async-start | bytes 1048576 | tf_op jit(solution)/shard_map/all_to_all | solution.py:115
  250.8 297.3 %all-reduce.3.cloned.1.call-start = ((), (), s32[]{:S(2)}) async-start(), calls=%async_computation.6 | async-start | bytes 7143424 | tf_op jit(solution)/shard_map/psum | solution.py:172
  256.5 13.5 %copy-start.16 = (bf16[2,256,256]{2,1,0:T(8,128)(2,1)S(1)}, bf16[2,256,256]{2,1,0:T(8,128)(2,1)}, u32[]{:S(2)}) copy-start(bf16[2,256,256]{2,1,0:T(8,128)(2,1)} %param.14) | copy-start | bytes 786436
  283.9 75.7 %copy-start.26 = (bf16[256,512]{1,0:T(8,128)(2,1)S(1)}, bf16[256,512]{1,0:T(8,128)(2,1)}, u32[]{:S(2)}) copy-start(bf16[256,512]{1,0:T(8,128)(2,1)} %get-tuple-element.33) | copy-start | bytes 786436
  (27 other events, 44.2 us)
Sparse Core Ops, SparseCore 0:
  284.1 263.9 all-reduce.2
where the time goes:
time: 574 us; the launch traced here: 562 us
  waiting for transfers between devices  253 us (44%)
  other arithmetic  76.6 us (13%)
  blocking collectives  75.1 us (13%)
  starting transfers between devices  55.3 us (10%)
  local copies, waits for them, and re-layouts  48.7 us (8%)
  matrix products  38.8 us (7%)
  between operations  14.9 us (3%)
    psum x1, waiting for transfers between devices, on_device(): lax.psum((grad_neigh, grad_self, grad_gate, grad_bias, grad_rel), ('hist'...  180 us
    psum x1, blocking collectives, on_device(): lax.psum((grad_neigh, grad_self, grad_gate, grad_bias, grad_rel), ('hist'...  75.1 us
    all_to_all x4, waiting for transfers between devices, on_device(): lax.all_to_all(replies.reshape(groups, bucket_slots, features), 'ent', sp...  41.4 us
    all_to_all x4, starting transfers between devices, on_device(): lax.all_to_all(replies.reshape(groups, bucket_slots, features), 'ent', sp...  27.6 us
    ppermute x3, waiting for transfers between devices, from_behind(): return lax.ppermute(block, axis, route)  23.2 us
    scatter-add x4, other arithmetic, on_device(): jax.ops.segment_sum(spread, rel_ids, num_segments=relation.shape[0])  21.2 us
    scatter-add x4, other arithmetic, on_device(): jnp.zeros((ent_rows, features), jnp.float32).at[src_ids]  18.1 us
    all_to_all x1, starting transfers between devices, on_device(): lax.all_to_all(targets, 'ent', split_axis=0, concat_axis=0, tiled=True)  13 us
  transfers between devices with their start and end apart: 10, of which 9 were waited for; matrix products, arithmetic and copies ran while one was open for 13% of the time, Pallas kernels for 0%

commit v1 on v0

v1 whole, which is shorter than its diff:
```python
import functools
import math

import jax
import jax.numpy as jnp
from jax import lax
from jax.experimental import pallas as pl
from jax.experimental.pallas import tpu as pltpu
from jax.sharding import PartitionSpec as P

MESH = pl.DeviceIdType.MESH
bf16 = jnp.bfloat16
f32 = jnp.float32

HIST = 4
ENT = 64
CORES, XS, ZS = 2, 4, 8
ROWS = 256
D = 512
HALF = 256
SLOTS = 512
NREL = 460
REL_PAD = 512
REL_ROWS = 464
O_GATE = 0
O_SELF = 2048
O_NEIGH = 4096
O_REL = 5120
O_BIAS = O_REL + 4 * REL_ROWS
GROWS = 7168
CORE_ROWS = GROWS // CORES
X_ROWS = CORE_ROWS // XS
Z_ROWS = X_ROWS // ZS


def nn(a, b):
    return jnp.dot(a, b, preferred_element_type=f32)


def nt(a, b):
    return lax.dot_general(a, b, (((1,), (1,)), ((), ())), preferred_element_type=f32)


def tn(a, b):
    return lax.dot_general(a, b, (((0,), (0,)), ((), ())), preferred_element_type=f32)


def iota(shape, dim):
    return lax.broadcasted_iota(jnp.int32, shape, dim)


def hot(cond):
    return jnp.where(cond, 1.0, 0.0).astype(bf16)


def split(v):
    high = v.astype(bf16)
    return high, (v - high.astype(f32)).astype(bf16)


def pack(m):
    low = m[:, :128].reshape(ENT, 8, 128)
    high = m[:, 128:].reshape(ENT, 8, 128)
    return jnp.concatenate([low, high], axis=1).astype(bf16)


def unpack(r):
    wide = r.astype(f32)
    low = wide[:, :8, :].reshape(SLOTS, 128)
    high = wide[:, 8:, :].reshape(SLOTS, 128)
    return jnp.concatenate([low, high], axis=1).astype(bf16)


def kernel(
    factor,
    states,
    w_neigh,
    w_self,
    w_gate,
    b_gate,
    relation,
    edge_src,
    edge_rel,
    edge_dst,
    counts,
    query_ent,
    query_rel,
    query_grad,
    out_states,
    out_neigh,
    out_self,
    out_gate,
    out_bias,
    out_rel,
    id_send,
    id_recv,
    f_send,
    f_recv,
    b_send,
    b_recv,
    c_send,
    c_recv,
    rel_pad,
    inputs,
    hot_src_t,
    hot_rel_t,
    hot_dst,
    returned,
    cot,
    keep,
    coef_gate,
    coef_pre,
    scaling,
    gate_low,
    pre_low,
    base,
    grads,
    core_recv,
    x_send,
    x_recv,
    z_send,
    z_recv,
    y_send,
    y_recv,
    gathered,
    id_sem,
    f_sem,
    b_sem,
    c_sem,
    core_sem,
    x_sem,
    z_sem,
    y_sem,
    gz_sem,
    gx_sem,
    gc_sem,
):
    hist = lax.axis_index("hist")
    me = lax.axis_index("ent")
    core = lax.rem(me, CORES)
    z = lax.rem(me // CORES, ZS)
    x = me // (CORES * ZS)

    barrier = pltpu.get_barrier_semaphore()

    def greet(i, carry):
        pl.semaphore_signal(
            barrier, inc=1, device_id={"ent": lax.rem(me + i, ENT)}, device_id_type=MESH
        )
        return carry

    lax.fori_loop(1, ENT, greet, 0)
    for i in range(1, HIST):
        pl.semaphore_signal(
            barrier, inc=1, device_id={"hist": lax.rem(hist + i, HIST)}, device_id_type=MESH
        )

    dst = edge_dst[...].astype(f32)
    own_slot = jnp.where((iota((ENT, SLOTS), 1) >> 3) == iota((ENT, SLOTS), 0), dst, 0.0)
    to_lane = hot((iota((SLOTS, 128), 0) & 7) == iota((SLOTS, 128), 1))
    target = nn(own_slot.astype(bf16), to_lane)
    own_count = jnp.where(
        iota((ENT, ENT), 0) == iota((ENT, ENT), 1), counts[...].astype(f32), 0.0
    )
    limit = nn(own_count.astype(bf16), jnp.ones((ENT, 128), bf16))
    id_send[...] = jnp.where(iota((ENT, 128), 1).astype(f32) < limit, target, -1.0)

    hot_src_t[...] = hot(iota((ROWS, SLOTS), 0) == edge_src[...])
    hot_rel_t[...] = hot(iota((REL_PAD, SLOTS), 0) == edge_rel[...])
    rel_pad[NREL // 16 * 16 :, :] = jnp.zeros((REL_PAD - NREL // 16 * 16, D), bf16)
    rel_pad[:NREL, :] = relation[...]
    inputs[...] = (
        tn(hot_src_t[...], states[0]) + tn(hot_rel_t[...], rel_pad[...])
    ).astype(bf16)

    pl.semaphore_wait(barrier, ENT - 1 + HIST - 1)

    def send_ids(i, carry):
        peer = lax.rem(me + i, ENT)
        pltpu.make_async_remote_copy(
            src_ref=id_send.at[pl.ds(peer, 1)],
            dst_ref=id_recv.at[pl.ds(me, 1)],
            send_sem=id_sem.at[0],
            recv_sem=id_sem.at[1],
            device_id={"ent": peer},
            device_id_type=MESH,
        ).start()
        return carry

    lax.fori_loop(1, ENT, send_ids, 0)
    id_recv[pl.ds(me, 1), :] = id_send[pl.ds(me, 1), :]

    def exchange(send, recv, sem, b):
        def step(i, carry):
            peer = lax.rem(me + i, ENT)
            pltpu.make_async_remote_copy(
                src_ref=send.at[b, peer],
                dst_ref=recv.at[b, me],
                send_sem=sem.at[0, b],
                recv_sem=sem.at[1, b],
                device_id={"ent": peer},
                device_id_type=MESH,
            ).start()
            return carry

        lax.fori_loop(1, ENT, step, 0)
        recv[b, me] = send[b, me]

    def wait_all(ref, sem):
        pltpu.make_async_copy(ref.at[pl.ds(0, ENT - 1)], ref.at[pl.ds(0, ENT - 1)], sem).wait()

    for b in range(2):
        cols = slice(b * HALF, (b + 1) * HALF)
        f_send[b] = pack(nn(inputs[:, cols], w_neigh[b]))
        exchange(f_send, f_recv, f_sem, b)

    hidden = states[0]
    base[...] = nn(hidden, w_self[...])
    gate = jax.nn.sigmoid(nn(hidden, w_gate[...]) + b_gate[...])
    keep[...] = 1.0 - gate

    grads[O_BIAS:, :] = jnp.zeros((GROWS - O_BIAS, 128), f32)

    @pl.when(hist == HIST - 1)
    def _():
        hot_query = hot(iota((ROWS, 128), 0) == query_ent[...])
        q = query_grad[...]
        high = q.astype(bf16)
        rest = q - high.astype(f32)
        middle, low = split(rest)
        cot[...] = nn(hot_query, high) + (nn(hot_query, middle) + nn(hot_query, low))

    wait_all(id_recv, id_sem.at[1])
    to_slot = hot((iota((SLOTS, ENT), 0) >> 3) == iota((SLOTS, ENT), 1))
    arrived = nn(to_slot, id_recv[...].astype(bf16))
    arrived = jnp.where(
        iota((SLOTS, 128), 1) == (iota((SLOTS, 128), 0) & 7), arrived, 0.0
    ).astype(bf16)
    ones = jnp.ones((ROWS, 128), bf16)
    hot_dst[...] = hot(nt(arrived, ones) == iota((SLOTS, ROWS), 1).astype(f32))
    hot_dst_t = hot(nt(ones, arrived) == iota((ROWS, SLOTS), 0).astype(f32))
    degree = nn(hot_dst_t, jnp.ones((SLOTS, HALF), bf16))
    scaling[...] = 1.0 / jnp.maximum(degree, 1.0)

    for b in range(2):
        cols = slice(b * HALF, (b + 1) * HALF)
        wait_all(f_recv.at[b], f_sem.at[1, b])
        summed = nn(hot_dst_t, unpack(f_recv[b]))
        pre_act = summed * scaling[...] + base[:, cols]
        sig = jax.nn.sigmoid(pre_act)
        shut = keep[:, cols]
        opened = 1.0 - shut
        coef_gate[:, cols] = (pre_act * sig - states[0, :, cols].astype(f32)) * opened * shut
        coef_pre[:, cols] = opened * (sig * (1.0 + pre_act * (1.0 - sig)))

    for b in range(2):
        cols = slice(b * HALF, (b + 1) * HALF)

        @pl.when(hist < HIST - 1)
        def _():
            pltpu.make_async_copy(c_recv.at[b], c_recv.at[b], c_sem.at[1, b]).wait()
            cot[:, cols] = c_recv[b].astype(f32)

        c = cot[:, cols]
        pre_term = c * coef_pre[:, cols]
        b_send[b] = pack(nn(hot_dst[...], (pre_term * scaling[...]).astype(bf16)))
        exchange(b_send, b_recv, b_sem, b)
        pre_low[:, cols] = pre_term.astype(bf16)
        gate_term = c * coef_gate[:, cols]
        gate_low[:, cols] = gate_term.astype(bf16)
        bias = jnp.sum(gate_term, axis=0, keepdims=True)
        for j in range(2):
            at = O_BIAS + 2 * b + j
            grads[at : at + 1, :] = bias[:, j * 128 : (j + 1) * 128]

    base[...] = (
        cot[...] * keep[...] + nt(gate_low[...], w_gate[...]) + nt(pre_low[...], w_self[...])
    )
    for start, low in ((O_GATE, gate_low), (O_SELF, pre_low)):
        total = tn(hidden, low[...])
        for j in range(4):
            grads[start + j * 512 : start + (j + 1) * 512, :] = total[:, j * 128 : (j + 1) * 128]

    for b in range(2):
        cols = slice(b * HALF, (b + 1) * HALF)
        wait_all(b_recv.at[b], b_sem.at[1, b])
        back = unpack(b_recv[b])
        returned[:, cols] = back
        high, low = split(nn(hot_src_t[...], back))
        result = base[:, cols] + (nt(high, w_neigh[b]) + nt(low, w_neigh[b]))
        out_states[0, :, cols] = result

        @pl.when(hist > 0)
        def _():
            c_send[b] = result.astype(bf16)
            pltpu.make_async_remote_copy(
                src_ref=c_send.at[b],
                dst_ref=c_recv.at[b],
                send_sem=c_sem.at[0, b],
                recv_sem=c_sem.at[1, b],
                device_id={"hist": hist - 1},
                device_id_type=MESH,
            ).start()

    for b in range(2):
        cols = slice(b * HALF, (b + 1) * HALF)
        back = returned[:, cols]
        total = tn(inputs[:, cols], back)
        high, low = split(nn(hot_rel_t[...], back))
        by_rel = nt(high, w_neigh[b]) + nt(low, w_neigh[b])
        for j in range(2):
            lanes = slice(j * 128, (j + 1) * 128)
            at = O_NEIGH + (2 * b + j) * 256
            grads[at : at + 256, :] = total[:, lanes]
            at = O_REL + (2 * b + j) * REL_ROWS
            grads[at : at + REL_ROWS, :] = by_rel[:REL_ROWS, lanes]

    @pl.when(hist == HIST - 1)
    def _():
        hot_query = hot(iota((REL_PAD, 128), 0) == query_rel[...])
        q = query_grad[...]
        high = q.astype(bf16)
        rest = q - high.astype(f32)
        middle, low = split(rest)
        part = nn(hot_query, high) + (nn(hot_query, middle) + nn(hot_query, low))
        for j in range(4):
            at = O_REL + j * REL_ROWS
            grads[at : at + REL_ROWS, :] += part[:REL_ROWS, j * 128 : (j + 1) * 128]

    def remote(src, dst, sem, i, where):
        copy = pltpu.make_async_remote_copy(
            src_ref=src,
            dst_ref=dst,
            send_sem=sem.at[0, i],
            recv_sem=sem.at[1, i],
            device_id=where,
            device_id_type=MESH,
        )
        copy.start()
        return copy

    other = 1 - core
    partner = me + 1 - 2 * core
    core_copy = remote(
        grads.at[pl.ds(pl.multiple_of(other * CORE_ROWS, CORE_ROWS), CORE_ROWS)],
        core_recv,
        core_sem,
        0,
        {"ent": partner},
    )
    core_copy.wait()
    mine = pl.multiple_of(core * CORE_ROWS, CORE_ROWS)
    x_send[...] = (
        (grads[pl.ds(mine, CORE_ROWS), :] + core_recv[...]).astype(bf16).reshape(XS, X_ROWS, 128)
    )
    copies = []
    for i in range(1, XS):
        there = lax.rem(x + i, XS)
        copies.append(
            remote(
                x_send.at[there],
                x_recv.at[x],
                x_sem,
                i,
                {"ent": me + (there - x) * (CORES * ZS)},
            )
        )
    part_rows = pl.ds(pl.multiple_of(mine + x * X_ROWS, X_ROWS), X_ROWS)
    here = pl.ds(pl.multiple_of(x * X_ROWS, X_ROWS), X_ROWS)
    total = grads[part_rows, :] + core_recv[here, :]
    for copy in copies:
        copy.wait()
    for i in range(1, XS):
        total = total + x_recv[lax.rem(x + i, XS)].astype(f32)
    z_send[...] = total.astype(bf16).reshape(ZS, Z_ROWS, 128)
    z_recv[z] = z_send[z]
    copies = []
    for i in range(1, ZS):
        there = lax.rem(z + i, ZS)
        copies.append(
            remote(
                z_send.at[there], z_recv.at[z], z_sem, i, {"ent": me + (there - z) * CORES}
            )
        )
    for copy in copies:
        copy.wait()
    shard = z_recv[0].astype(f32)
    for i in range(1, ZS):
        shard = shard + z_recv[i].astype(f32)
    y_send[...] = shard
    copies = []
    for i in range(1, HIST):
        copies.append(
            remote(y_send, y_recv.at[hist], y_sem, i, {"hist": lax.rem(hist + i, HIST)})
        )
    y_recv[hist] = shard
    for copy in copies:
        copy.wait()
    shard = (y_recv[0] + y_recv[1]) + (y_recv[2] + y_recv[3])

    start = pl.multiple_of(mine + x * X_ROWS + z * Z_ROWS, Z_ROWS)
    own = gathered.at[pl.ds(start, Z_ROWS)]
    own[...] = shard.astype(bf16)
    copies = []
    for i in range(1, ZS):
        there = lax.rem(z + i, ZS)
        copies.append(remote(own, own, gz_sem, i, {"ent": me + (there - z) * CORES}))
    for copy in copies:
        copy.wait()
    own = gathered.at[part_rows]
    copies = []
    for i in range(1, XS):
        there = lax.rem(x + i, XS)
        copies.append(remote(own, own, gx_sem, i, {"ent": me + (there - x) * (CORES * ZS)}))
    for copy in copies:
        copy.wait()
    own = gathered.at[pl.ds(mine, CORE_ROWS)]
    remote(own, own, gc_sem, 0, {"ent": partner}).wait()

    for j in range(4):
        lanes = slice(j * 128, (j + 1) * 128)
        for ref, first, rows in (
            (out_gate, O_GATE, 512),
            (out_self, O_SELF, 512),
        ):
            at = first + j * rows
            ref[:, lanes] = gathered[at : at + rows, :].astype(f32) * factor
        at = O_NEIGH + j * 256
        out_neigh[j // 2, :, (j % 2) * 128 : (j % 2 + 1) * 128] = (
            gathered[at : at + 256, :].astype(f32) * factor
        )
        at = O_REL + j * REL_ROWS
        out_rel[:, lanes] = gathered[at : at + REL_ROWS, :].astype(f32)[:NREL] * factor
    bias = gathered[O_BIAS : O_BIAS + 16, :].astype(f32) * factor
    for j in range(4):
        out_bias[:, j * 128 : (j + 1) * 128] = bias[j : j + 1, :]

    wait_all(id_send, id_sem.at[0])
    for b in range(2):
        wait_all(f_send.at[b], f_sem.at[0, b])
        wait_all(b_send.at[b], b_sem.at[0, b])

        @pl.when(hist > 0)
        def _():
            pltpu.make_async_copy(c_send.at[b], c_send.at[b], c_sem.at[0, b]).wait()


def on_device(
    states,
    w_neigh,
    w_self,
    w_gate,
    b_gate,
    relation,
    edge_src,
    edge_rel,
    edge_dst,
    send_counts,
    query_ent,
    query_rel,
    query_grad,
):
    factor = 1.0 / math.sqrt(HIST * ENT * ROWS)
    vmem = pl.BlockSpec(memory_space=pltpu.VMEM)
    dma = pltpu.SemaphoreType.DMA
    shape = jax.ShapeDtypeStruct
    outs = pl.pallas_call(
        functools.partial(kernel, factor),
        out_shape=(
            shape((1, ROWS, D), f32),
            shape((2, HALF, HALF), f32),
            shape((D, D), f32),
            shape((D, D), f32),
            shape((1, D), f32),
            shape((NREL, D), f32),
        ),
        in_specs=[vmem] * 13,
        out_specs=(vmem,) * 6,
        scratch_shapes=[
            pltpu.VMEM((ENT, 128), f32),
            pltpu.VMEM((ENT, 128), f32),
            pltpu.VMEM((2, ENT, 16, 128), bf16),
            pltpu.VMEM((2, ENT, 16, 128), bf16),
            pltpu.VMEM((2, ENT, 16, 128), bf16),
            pltpu.VMEM((2, ENT, 16, 128), bf16),
            pltpu.VMEM((2, ROWS, HALF), bf16),
            pltpu.VMEM((2, ROWS, HALF), bf16),
            pltpu.VMEM((REL_PAD, D), bf16),
            pltpu.VMEM((SLOTS, D), bf16),
            pltpu.VMEM((ROWS, SLOTS), bf16),
            pltpu.VMEM((REL_PAD, SLOTS), bf16),
            pltpu.VMEM((SLOTS, ROWS), bf16),
            pltpu.VMEM((SLOTS, D), bf16),
            pltpu.VMEM((ROWS, D), f32),
            pltpu.VMEM((ROWS, D), f32),
            pltpu.VMEM((ROWS, D), f32),
            pltpu.VMEM((ROWS, D), f32),
            pltpu.VMEM((ROWS, HALF), f32),
            pltpu.VMEM((ROWS, D), bf16),
            pltpu.VMEM((ROWS, D), bf16),
            pltpu.VMEM((ROWS, D), f32),
            pltpu.VMEM((GROWS, 128), f32),
            pltpu.VMEM((CORE_ROWS, 128), f32),
            pltpu.VMEM((XS, X_ROWS, 128), bf16),
            pltpu.VMEM((XS, X_ROWS, 128), bf16),
            pltpu.VMEM((ZS, Z_ROWS, 128), bf16),
            pltpu.VMEM((ZS, Z_ROWS, 128), bf16),
            pltpu.VMEM((Z_ROWS, 128), f32),
            pltpu.VMEM((HIST, Z_ROWS, 128), f32),
            pltpu.VMEM((GROWS, 128), bf16),
            dma((2,)),
            dma((2, 2)),
            dma((2, 2)),
            dma((2, 2)),
            dma((2, 1)),
            dma((2, XS)),
            dma((2, ZS)),
            dma((2, HIST)),
            dma((2, ZS)),
            dma((2, XS)),
            dma((2, 1)),
        ],
        compiler_params=pltpu.CompilerParams(
            collective_id=0, has_side_effects=True, vmem_limit_bytes=50 << 20
        ),
        name="encoder_backward",
    )(
        states,
        w_neigh,
        w_self,
        w_gate,
        b_gate.reshape(1, D),
        relation,
        edge_src,
        edge_rel,
        edge_dst,
        send_counts,
        query_ent.reshape(1, 128),
        query_rel.reshape(1, 128),
        query_grad,
    )
    result, grad_neigh, grad_self, grad_gate, grad_bias, grad_rel = outs
    return result, grad_neigh, grad_self, grad_gate, grad_bias.reshape(D), grad_rel


def solution(mesh):
    return jax.shard_map(
        on_device,
        mesh=mesh,
        in_specs=(
            P("hist", "ent", None),
            P(),
            P(),
            P(),
            P(),
            P(),
            P("hist", "ent"),
            P("hist", "ent"),
            P("hist", "ent"),
            P("hist", "ent"),
            P("ent"),
            P("ent"),
            P("ent", None),
        ),
        out_specs=(P("hist", "ent", None), P(), P(), P(), P(), P()),
        check_vma=False,
    )
```

time: 574 us -> 157 us (0.27); the launches traced: 562 us -> 157 us
  waiting for transfers between devices: 253 us -> 0 us
  Pallas kernels: 0 us -> 142 us
  other arithmetic: 76.6 us -> 0 us
  blocking collectives: 75.1 us -> 0 us
  starting transfers between devices: 55.3 us -> 0 us
  matrix products: 38.8 us -> 0 us
  local copies, waits for them, and re-layouts: 48.7 us -> 13.7 us
  between operations: 14.9 us -> 0.71 us
    psum x1 -> x0, waiting for transfers between devices: 180 us -> none  [on_device(): lax.psum((grad_neigh, grad_self, grad_gate, grad_bias, grad_rel), ('hist'...]
    pallas_call x0 -> x1, Pallas kernels: none -> 142 us  [on_device(): pl.pallas_call(functools.partial(kernel, factor), out_shape=(shape((1, RO...]
    psum x1 -> x0, blocking collectives: 75.1 us -> none  [on_device(): lax.psum((grad_neigh, grad_self, grad_gate, grad_bias, grad_rel), ('hist'...]
    all_to_all x6 -> x0, starting transfers between devices: 51 us -> none  [the longest x4 27.6 us: on_device(): lax.all_to_all(replies.reshape(groups, bucket_slots, features), 'ent', sp...]
    scatter-add x11 -> x0, other arithmetic: 50.1 us -> none  [the longest x4 21.2 us: on_device(): jax.ops.segment_sum(spread, rel_ids, num_segments=relation.shape[0])]
    all_to_all x6 -> x0, waiting for transfers between devices: 49.3 us -> none  [the longest x4 41.4 us: on_device(): lax.all_to_all(replies.reshape(groups, bucket_slots, features), 'ent', sp...]
    dot_general x28 -> x0, matrix products: 38.8 us -> none  [the longest x4 9.05 us: on_device(): lax.dot_general(hidden, gate_low, contract, preferred_element_type=jnp.fl...]
    ppermute x3 -> x0, waiting for transfers between devices: 23.2 us -> none  [from_behind(): return lax.ppermute(block, axis, route)]
  transfers between devices with their start and end apart: 10 -> 0, of which waited for: 9 -> 0; matrix products, arithmetic and copies ran while one was open for 13% -> 0% of each run, Pallas kernels for 0% -> 0%
where the time goes in v1:
time: 157 us
  Pallas kernels  142 us (90%)
  local copies, waits for them, and re-layouts  13.7 us (9%)
    pallas_call x1, Pallas kernels, on_device(): pl.pallas_call(functools.partial(kernel, factor), out_shape=(shape((1, RO...  142 us
    unnamed x38, local copies, waits for them, and re-layouts  13.7 us

profile of v1, /device:TPU:1, one launch (start us, length us, event | category | flops | bytes accessed | tf_op | source)
XLA Modules:
  0.0 156.5 jit_solution(3525393875193825014)
XLA Ops:
  0.6 0.0 copy-start.7
  0.6 0.0 copy-start.6
  0.7 0.0 copy-start.10
  0.7 0.0 copy-start.11
  0.7 0.6 copy-done.7
  1.3 0.0 copy-done.6
  1.3 0.0 copy-done.12
  1.4 1.0 copy-done
  2.4 1.0 copy-done.1
  3.4 1.0 copy-done.2
  4.5 0.9 copy-done.3
  5.4 0.9 copy-done.4
  6.4 0.9 copy-done.5
  7.3 0.7 copy-done.8
  8.0 0.7 copy-done.9
  8.7 142.1 %encoder_backward.1 = (f32[1,256,512]{2,1,0:T(8,128)S(1)}, f32[2,256,256]{2,1,0:T(8,128)S(1)}, f32[512,512]{1,0:T(8,128)}, f32[512,512]{1,0:T(8,128)}, f32[1,512]{1,0:T(1,128)S(1)}, /*index=5*/f32[460,512]{1,0:T(8,128)}) custom-call(bf16[1,256,512]{2,1,0:T(8,128)(2,1)S(1)} %copy-done.3, bf16[2,256,256]{2,1,0:T(8,128)(2,1)S(1)} %copy-done.4, ...), custom_call_target="tpu_custom_call" | custom-call | tf_op jit(solution)/shard_map/encoder_backward/pallas_call | solution.py:467
  150.8 0.8 copy.25
  151.6 0.8 copy.26
  152.4 1.0 copy.27
  153.4 0.6 copy-done.13
  154.0 1.0 copy.28
  155.0 0.6 copy.29
  155.6 0.0 copy-done.15
  155.6 0.9 copy.30
  (15 shorter events, 0.0 us)
Async XLA Ops:
  0.6 0.7 copy-start.7
  0.6 0.7 copy-start.6
  0.7 0.7 copy-start.10
  0.7 0.7 copy-start.11
  0.7 0.7 copy-start.12
  1.4 1.0 copy-start
  2.4 1.0 copy-start.1
  3.4 1.0 copy-start.2
  4.5 0.9 copy-start.3
  5.4 0.9 copy-start.4
  6.4 0.9 copy-start.5
  7.3 0.7 copy-start.8
  8.0 0.7 copy-start.9
  150.8 1.6 %copy-start.14 = (f32[512,512]{1,0:T(8,128)S(1)}, f32[512,512]{1,0:T(8,128)}, u32[]{:S(2)}) copy-start(f32[512,512]{1,0:T(8,128)} %get-tuple-element.26) | copy-start | bytes 3145732
  152.4 1.6 %copy-start.13 = (f32[512,512]{1,0:T(8,128)S(1)}, f32[512,512]{1,0:T(8,128)}, u32[]{:S(2)}) copy-start(f32[512,512]{1,0:T(8,128)} %get-tuple-element.27) | copy-start | bytes 3145732
  154.0 1.6 %copy-start.15 = (f32[460,512]{1,0:T(8,128)S(1)}, f32[460,512]{1,0:T(8,128)}, u32[]{:S(2)}) copy-start(f32[460,512]{1,0:T(8,128)} %get-tuple-element.29) | copy-start | bytes 2826244

commit v2 on v1

v2 whole, which is shorter than its diff:
```python
import functools
import math

import jax
import jax.numpy as jnp
from jax import lax
from jax.experimental import pallas as pl
from jax.experimental.pallas import tpu as pltpu
from jax.sharding import PartitionSpec as P

MESH = pl.DeviceIdType.MESH
bf16 = jnp.bfloat16
f32 = jnp.float32

HIST = 4
ENT = 64
CORES, XS, ZS = 2, 4, 8
ROWS = 256
D = 512
HALF = 256
QUART = 128
SLOTS = 512
NREL = 460
REL_PAD = 512
R_GATE, R_SELF, R_NEIGH, R_REL, R_QUERY = 0, 8, 16, 24, 32
SHARD = 40
KEPT = 32
BIAS_ROW = 508


def nn(a, b):
    return jnp.dot(a, b, preferred_element_type=f32)


def nt(a, b):
    return lax.dot_general(a, b, (((1,), (1,)), ((), ())), preferred_element_type=f32)


def tn(a, b):
    return lax.dot_general(a, b, (((0,), (0,)), ((), ())), preferred_element_type=f32)


def iota(shape, dim):
    return lax.broadcasted_iota(jnp.int32, shape, dim)


def hot(cond):
    return jnp.where(cond, 1.0, 0.0).astype(bf16)


def split(v):
    high = v.astype(bf16)
    return high, (v - high.astype(f32)).astype(bf16)


def split3(v):
    high = v.astype(bf16)
    middle, low = split(v - high.astype(f32))
    return high, middle, low


def by_shard(v):
    return v.reshape(-1, 8, QUART)


def pack(m):
    return m.reshape(ENT, 8, QUART).astype(bf16)


def unpack(r):
    return r.astype(f32).reshape(SLOTS, QUART).astype(bf16)


def kernel(
    states_in,
    w_neigh_in,
    w_self_in,
    w_gate_in,
    b_gate_in,
    relation_in,
    edge_src_in,
    edge_rel_in,
    edge_dst_in,
    counts_in,
    query_ent_in,
    query_rel_in,
    query_grad_in,
    gathered,
    result,
    states,
    w_cols,
    w_own,
    w_other,
    w_self,
    w_gate,
    b_gate,
    relation,
    ids,
    edge_dst,
    counts,
    query_ent,
    query_rel,
    query_grad,
    id_send,
    id_recv,
    rel_block,
    inputs,
    hot_src_t,
    hot_rel_t,
    hot_dst,
    f_send,
    f_recv,
    b_send,
    b_recv,
    cot,
    keep,
    coef_gate,
    coef_pre,
    scaling,
    bias,
    part,
    part_send,
    part_recv,
    sum_send,
    sum_recv,
    res_send,
    grads,
    core_recv,
    x_send,
    x_recv,
    z_send,
    z_recv,
    rel_send,
    rel_recv,
    fetch_sem,
    id_sem,
    fwd_id_sem,
    st_sem,
    ids_sem,
    f_sem,
    b_sem,
    part_sem,
    sum_sem,
    res_sem,
    core_sem,
    x_sem,
    z_sem,
    rel_sem,
    gy_sem,
    gz_sem,
    gx_sem,
    gc_sem,
):
    hist = lax.axis_index("hist")
    me = lax.axis_index("ent")
    core = lax.rem(me, CORES)
    z = lax.rem(me // CORES, ZS)
    x = me // (CORES * ZS)
    block = hist // 2
    side = lax.rem(hist, 2)
    mate = hist + 1 - 2 * side

    top = HIST - 1
    barrier = pltpu.get_barrier_semaphore()

    def greet(i, carry):
        pl.semaphore_signal(
            barrier, inc=1, device_id={"ent": lax.rem(me + i, ENT)}, device_id_type=MESH
        )
        return carry

    cols = pl.ds(pl.multiple_of(hist * QUART, QUART), QUART)
    near = pl.ds(pl.multiple_of(side * QUART, QUART), QUART)
    far = pl.ds(pl.multiple_of((1 - side) * QUART, QUART), QUART)
    fetched = []

    def fetch(src, dst):
        copy = pltpu.make_async_copy(src, dst, fetch_sem.at[len(fetched)])
        copy.start()
        fetched.append(copy)

    fetch(edge_dst_in, edge_dst)
    fetch(counts_in, counts)
    fetch(edge_src_in, ids.at[hist, pl.ds(0, 1)])
    fetch(edge_rel_in, ids.at[hist, pl.ds(1, 1)])
    fetch(states_in.at[0, :, pl.ds(0, HALF)], states.at[hist, 0])
    fetch(states_in.at[0, :, pl.ds(HALF, HALF)], states.at[hist, 1])
    fetch(relation_in, relation)
    fetch(w_neigh_in.at[block, :, near], w_cols)
    fetch(w_neigh_in.at[block, near, near], w_own)
    fetch(w_neigh_in.at[block, near, far], w_other)
    fetch(w_self_in.at[:, cols], w_self)
    fetch(w_gate_in.at[:, cols], w_gate)
    fetch(b_gate_in.at[:, cols], b_gate)
    fetch(query_ent_in, query_ent)
    fetch(query_rel_in, query_rel)
    fetch(query_grad_in.at[:, cols], query_grad)

    lax.fori_loop(1, ENT, greet, 0)
    for i in range(1, HIST):
        pl.semaphore_signal(
            barrier, inc=1, device_id={"hist": lax.rem(hist + i, HIST)}, device_id_type=MESH
        )

    fetched[0].wait()
    fetched[1].wait()
    dst = edge_dst[...].astype(f32)
    own_slot = jnp.where((iota((ENT, SLOTS), 1) >> 3) == iota((ENT, SLOTS), 0), dst, 0.0)
    to_lane = hot((iota((SLOTS, 128), 0) & 7) == iota((SLOTS, 128), 1))
    target = nn(own_slot.astype(bf16), to_lane)
    own_count = jnp.where(
        iota((ENT, ENT), 0) == iota((ENT, ENT), 1), counts[...].astype(f32), 0.0
    )
    limit = nn(own_count.astype(bf16), jnp.ones((ENT, 128), bf16))
    id_send[...] = jnp.where(iota((ENT, 128), 1).astype(f32) < limit, target, -1.0)

    for i in range(2, 6):
        fetched[i].wait()

    def wait_bytes(ref, sem):
        pltpu.make_async_copy(ref, ref, sem).wait()

    def remote(src, dst, send, recv, where):
        copy = pltpu.make_async_remote_copy(
            src_ref=src,
            dst_ref=dst,
            send_sem=send,
            recv_sem=recv,
            device_id=where,
            device_id_type=MESH,
        )
        copy.start()
        return copy

    def share_states(t):
        @pl.when(hist == t)
        def _():
            order = [(t + 3) % HIST, (t + 1) % HIST, (t + 2) % HIST]
            for p in order:
                remote(
                    ids.at[t], ids.at[t], ids_sem.at[0, t], ids_sem.at[1, t], {"hist": p}
                )
            for first in (True, False):
                for p in order:
                    b = p // 2 if first else 1 - p // 2
                    remote(
                        states.at[t, b],
                        states.at[t, b],
                        st_sem.at[0, t],
                        st_sem.at[1 + b, t],
                        {"hist": p},
                    )

    pl.semaphore_wait(barrier, ENT - 1 + HIST - 1)
    share_states(HIST - 1)

    def send_ids(i, carry):
        peer = lax.rem(me + i, ENT)
        remote(
            id_send.at[pl.ds(peer, 1)],
            id_recv.at[hist, pl.ds(me, 1)],
            id_sem.at[0],
            id_sem.at[1],
            {"ent": peer},
        )
        return carry

    lax.fori_loop(1, ENT, send_ids, 0)
    id_recv[hist, pl.ds(me, 1), :] = id_send[pl.ds(me, 1), :]

    def exchange(send, recv, sem, t):
        def step(i, carry):
            peer = lax.rem(me + i, ENT)
            remote(send.at[t, peer], recv.at[t, me], sem.at[0, t], sem.at[1, t], {"ent": peer})
            return carry

        lax.fori_loop(1, ENT, step, 0)
        recv[t, me] = send[t, me]

    others = pl.ds(0, ENT - 1)

    for i in range(6, len(fetched)):
        fetched[i].wait()
    rel_block[NREL // 16 * 16 :, :] = jnp.zeros((REL_PAD - NREL // 16 * 16, HALF), bf16)
    rel_block[:NREL, :] = relation[:, pl.ds(pl.multiple_of(block * HALF, HALF), HALF)]

    q_parts = split3(query_grad[...])
    hot_query = hot(iota((ROWS, 128), 0) == query_ent[...])
    cot[...] = nn(hot_query, q_parts[0]) + (nn(hot_query, q_parts[1]) + nn(hot_query, q_parts[2]))
    hot_query = hot(iota((REL_PAD, 128), 0) == query_rel[...])
    grads[:, R_QUERY : R_QUERY + 8, :] = by_shard(
        nn(hot_query, q_parts[0]) + (nn(hot_query, q_parts[1]) + nn(hot_query, q_parts[2]))
    )
    grads[32:, R_NEIGH : R_NEIGH + 8, :] = jnp.zeros((32, 8, QUART), f32)

    def forward_messages(t):
        @pl.when(hist != t)
        def _():
            wait_bytes(ids.at[t], ids_sem.at[1, t])
            wait_bytes(states.at[t, block], st_sem.at[1 + block, t])

        if t == top:
            share_states(t - 1)
        hot_src_t[t] = hot(iota((ROWS, SLOTS), 0) == ids[t, 0:1, :])
        hot_rel_t[t] = hot(iota((REL_PAD, SLOTS), 0) == ids[t, 1:2, :])
        inputs[t] = (
            tn(hot_src_t[t], states[t, block]) + tn(hot_rel_t[t], rel_block[...])
        ).astype(bf16)
        f_send[t] = pack(nn(inputs[t], w_cols[...]))
        exchange(f_send, f_recv, f_sem, t)

    def forward_rest(t):
        @pl.when(hist != t)
        def _():
            wait_bytes(states.at[t, 1 - block], st_sem.at[2 - block, t])

        logit = nn(states[t, 0], w_gate[:HALF, :]) + nn(states[t, 1], w_gate[HALF:, :])
        dense = nn(states[t, 0], w_self[:HALF, :]) + nn(states[t, 1], w_self[HALF:, :])
        opened = jax.nn.sigmoid(logit + b_gate[...])
        shut = 1.0 - opened

        @pl.when(hist != t)
        def _():
            wait_bytes(id_recv.at[t], fwd_id_sem.at[1, t])

        to_slot = hot((iota((SLOTS, ENT), 0) >> 3) == iota((SLOTS, ENT), 1))
        arrived = nn(to_slot, id_recv[t].astype(bf16))
        arrived = jnp.where(
            iota((SLOTS, 128), 1) == (iota((SLOTS, 128), 0) & 7), arrived, 0.0
        ).astype(bf16)
        ones = jnp.ones((ROWS, 128), bf16)
        hot_dst[t] = hot(nt(arrived, ones) == iota((SLOTS, ROWS), 1).astype(f32))
        hot_dst_t = hot(nt(ones, arrived) == iota((ROWS, SLOTS), 0).astype(f32))
        degree = nn(hot_dst_t, jnp.ones((SLOTS, QUART), bf16))
        scale = 1.0 / jnp.maximum(degree, 1.0)
        scaling[t] = scale
        wait_bytes(f_recv.at[t, others], f_sem.at[1, t])
        pre_act = nn(hot_dst_t, unpack(f_recv[t])) * scale + dense
        sig = jax.nn.sigmoid(pre_act)
        keep[t] = shut
        own = states[t, block, :, near].astype(f32)
        coef_gate[t] = (pre_act * sig - own) * opened * shut
        coef_pre[t] = opened * (sig * (1.0 + pre_act * (1.0 - sig)))

    forward_messages(top)
    wait_bytes(id_recv.at[hist, others], id_sem.at[1])
    for i in range(1, HIST):
        remote(
            id_recv.at[hist],
            id_recv.at[hist],
            fwd_id_sem.at[0, hist],
            fwd_id_sem.at[1, hist],
            {"hist": lax.rem(hist + i, HIST)},
        )
    for t in range(top - 1):
        share_states(t)
    forward_rest(top)

    def add_grads(at, value, t, shards=ENT):
        if t == top:
            grads[:shards, at : at + 8, :] = by_shard(value)
        else:
            grads[:shards, at : at + 8, :] += by_shard(value)

    def returned_grads(t):
        back = unpack(b_recv[t])
        add_grads(R_NEIGH, tn(inputs[t], back), t, 32)
        add_grads(R_REL, nn(hot_rel_t[t], back), t)

    for t in range(top, -1, -1):
        c = cot[...]
        pre_term = c * coef_pre[t]
        b_send[t] = pack(nn(hot_dst[t], (pre_term * scaling[t]).astype(bf16)))
        exchange(b_send, b_recv, b_sem, t)
        gate_term = c * coef_gate[t]
        gate_low = gate_term.astype(bf16)
        pre_low = pre_term.astype(bf16)
        for j in range(4):
            rows = slice(j * QUART, (j + 1) * QUART)
            piece = nt(gate_low, w_gate[rows, :]) + nt(pre_low, w_self[rows, :])
            part[j] = piece
            part_send[t, j] = piece.astype(bf16)
        for i in range(1, HIST):
            there = lax.rem(hist + i, HIST)
            remote(
                part_send.at[t, there],
                part_recv.at[t, hist],
                part_sem.at[0, t],
                part_sem.at[1, t],
                {"hist": there},
            )
        if t > 0:
            forward_messages(t - 1)
        down = jnp.sum(gate_term, axis=0, keepdims=True)
        bias[...] = down if t == top else bias[...] + down
        for at, low in ((R_GATE, gate_low), (R_SELF, pre_low)):
            add_grads(
                at, jnp.concatenate([tn(states[t, 0], low), tn(states[t, 1], low)], axis=0), t
            )
        if t < top:
            returned_grads(t + 1)

        wait_bytes(b_recv.at[t, others], b_sem.at[1, t])
        high, low = split(nn(hot_src_t[t], unpack(b_recv[t])))
        sum_send[t] = high
        remote(
            sum_send.at[t], sum_recv.at[t], sum_sem.at[0, t], sum_sem.at[1, t], {"hist": mate}
        )
        near_part = nt(high, w_own[...]) + nt(low, w_own[...]) + c * keep[t] + part[hist]
        if t > 0:
            forward_rest(t - 1)
        wait_bytes(part_recv.at[t, pl.ds(0, HIST - 1)], part_sem.at[1, t])
        for i in range(1, HIST):
            near_part = near_part + part_recv[t, lax.rem(hist + i, HIST)].astype(f32)
        wait_bytes(sum_recv.at[t], sum_sem.at[1, t])
        c = near_part + nt(sum_recv[t], w_other[...])
        cot[...] = c
        res_send[t] = c.astype(bf16)

        @pl.when(hist == t)
        def _():
            result[t] = res_send[t]

        @pl.when(hist != t)
        def _():
            remote(
                res_send.at[t],
                result.at[hist],
                res_sem.at[0],
                res_sem.at[1],
                {"hist": t},
            )

    returned_grads(0)
    grads[BIAS_ROW // 8, R_QUERY + BIAS_ROW % 8 : R_QUERY + BIAS_ROW % 8 + 1, :] = bias[...]

    partner = me + 1 - 2 * core
    half = ENT // CORES
    mine = pl.multiple_of(core * half, half)
    remote(
        grads.at[pl.ds(pl.multiple_of((1 - core) * half, half), half)],
        core_recv,
        core_sem.at[0],
        core_sem.at[1],
        {"ent": partner},
    ).wait()
    x_send[...] = (grads[pl.ds(mine, half)] + core_recv[...]).astype(bf16).reshape(
        XS, ZS, SHARD, QUART
    )
    copies = []
    for i in range(1, XS):
        there = lax.rem(x + i, XS)
        copies.append(
            remote(
                x_send.at[there],
                x_recv.at[x],
                x_sem.at[0, i],
                x_sem.at[1, i],
                {"ent": me + (there - x) * (CORES * ZS)},
            )
        )
    total = grads[pl.ds(mine + x * ZS, ZS)] + core_recv[pl.ds(x * ZS, ZS)]
    for copy in copies:
        copy.wait()
    for i in range(1, XS):
        total = total + x_recv[lax.rem(x + i, XS)].astype(f32)
    z_send[...] = total
    copies = []
    for i in range(1, ZS):
        there = lax.rem(z + i, ZS)
        copies.append(
            remote(
                z_send.at[there],
                z_recv.at[z],
                z_sem.at[0, i],
                z_sem.at[1, i],
                {"ent": me + (there - z) * CORES},
            )
        )
    shard = z_send[z]
    for copy in copies:
        copy.wait()
    for i in range(1, ZS):
        shard = shard + z_recv[lax.rem(z + i, ZS)]

    rel_send[...] = shard[R_REL : R_REL + 8, :]
    remote(rel_send, rel_recv, rel_sem.at[0], rel_sem.at[1], {"hist": mate}).wait()
    by_rel = shard[R_QUERY : R_QUERY + 8, :]
    for v, w in ((rel_send[...], w_own), (rel_recv[...], w_other)):
        high = v.astype(bf16).astype(f32)
        both = nt(jnp.concatenate([high, v - high], axis=0).astype(bf16), w[...])
        by_rel = by_rel + (both[:8, :] + both[8:, :])

    place = mine + x * ZS + z
    gathered[place, hist] = jnp.concatenate([shard[:R_REL, :], by_rel], axis=0).astype(bf16)
    own = gathered.at[place, hist]
    copies = []
    for i in range(1, HIST):
        there = lax.rem(hist + i, HIST)
        copies.append(remote(own, own, gy_sem.at[0, i], gy_sem.at[1, i], {"hist": there}))
    for copy in copies:
        copy.wait()
    own = gathered.at[place]
    copies = []
    for i in range(1, ZS):
        there = lax.rem(z + i, ZS)
        copies.append(
            remote(own, own, gz_sem.at[0, i], gz_sem.at[1, i], {"ent": me + (there - z) * CORES})
        )
    for copy in copies:
        copy.wait()
    own = gathered.at[pl.ds(mine + x * ZS, ZS)]
    copies = []
    for i in range(1, XS):
        there = lax.rem(x + i, XS)
        copies.append(
            remote(
                own,
                own,
                gx_sem.at[0, i],
                gx_sem.at[1, i],
                {"ent": me + (there - x) * (CORES * ZS)},
            )
        )
    for copy in copies:
        copy.wait()
    own = gathered.at[pl.ds(mine, half)]
    remote(own, own, gc_sem.at[0], gc_sem.at[1], {"ent": partner}).wait()

    three = pl.ds(0, HIST - 1)
    wait_bytes(result.at[three], res_sem.at[1])
    wait_bytes(res_send.at[three], res_sem.at[0])
    wait_bytes(id_send.at[others], id_sem.at[0])
    wait_bytes(id_recv.at[three], fwd_id_sem.at[0, hist])
    wait_bytes(ids.at[three], ids_sem.at[0, hist])
    wait_bytes(states.at[three], st_sem.at[0, hist])
    for t in range(HIST):
        wait_bytes(f_send.at[t, others], f_sem.at[0, t])
        wait_bytes(b_send.at[t, others], b_sem.at[0, t])
        wait_bytes(part_send.at[t, three], part_sem.at[0, t])
        wait_bytes(sum_send.at[t], sum_sem.at[0, t])


def unfold(factor, gathered, result, out_states, out_neigh, out_self, out_gate, out_bias, out_rel):
    for h in range(HIST):
        lanes = slice(h * QUART, (h + 1) * QUART)
        out_states[0, :, lanes] = result[h].astype(f32)
        rows = gathered[:, h].astype(f32) * factor
        out_gate[:, lanes] = rows[:, R_GATE : R_GATE + 8, :].reshape(D, QUART)
        out_self[:, lanes] = rows[:, R_SELF : R_SELF + 8, :].reshape(D, QUART)
        out_neigh[h // 2, :, (h % 2) * QUART : (h % 2 + 1) * QUART] = rows[
            :32, R_NEIGH : R_NEIGH + 8, :
        ].reshape(HALF, QUART)
        by_rel = rows[:, R_REL : R_REL + 8, :].reshape(REL_PAD, QUART)
        out_rel[:, lanes] = by_rel[:NREL, :]
        out_bias[:, lanes] = by_rel[BIAS_ROW : BIAS_ROW + 1, :]


def on_device(
    states,
    w_neigh,
    w_self,
    w_gate,
    b_gate,
    relation,
    edge_src,
    edge_rel,
    edge_dst,
    send_counts,
    query_ent,
    query_rel,
    query_grad,
):
    factor = 1.0 / math.sqrt(HIST * ENT * ROWS)
    vmem = pl.BlockSpec(memory_space=pltpu.VMEM)
    anywhere = pl.BlockSpec(memory_space=pl.ANY)
    dma = pltpu.SemaphoreType.DMA
    shape = jax.ShapeDtypeStruct
    v = pltpu.VMEM
    i32 = jnp.int32
    gathered, result = pl.pallas_call(
        kernel,
        out_shape=(
            shape((ENT, HIST, KEPT, QUART), bf16),
            shape((HIST, ROWS, QUART), bf16),
        ),
        in_specs=[anywhere] * 13,
        out_specs=(vmem,) * 2,
        scratch_shapes=[
            v((HIST, 2, ROWS, HALF), bf16),
            v((HALF, QUART), bf16),
            v((QUART, QUART), bf16),
            v((QUART, QUART), bf16),
            v((D, QUART), bf16),
            v((D, QUART), bf16),
            v((1, QUART), f32),
            v((NREL, D), bf16),
            v((HIST, 8, SLOTS), i32),
            v((1, SLOTS), i32),
            v((1, ENT), i32),
            v((1, 128), i32),
            v((1, 128), i32),
            v((128, QUART), f32),
            v((ENT, 128), f32),
            v((HIST, ENT, 128), f32),
            v((REL_PAD, HALF), bf16),
            v((HIST, SLOTS, HALF), bf16),
            v((HIST, ROWS, SLOTS), bf16),
            v((HIST, REL_PAD, SLOTS), bf16),
            v((HIST, SLOTS, ROWS), bf16),
            v((HIST, ENT, 8, QUART), bf16),
            v((HIST, ENT, 8, QUART), bf16),
            v((HIST, ENT, 8, QUART), bf16),
            v((HIST, ENT, 8, QUART), bf16),
            v((ROWS, QUART), f32),
            v((HIST, ROWS, QUART), f32),
            v((HIST, ROWS, QUART), f32),
            v((HIST, ROWS, QUART), f32),
            v((HIST, ROWS, QUART), f32),
            v((1, QUART), f32),
            v((HIST, ROWS, QUART), f32),
            v((HIST, HIST, ROWS, QUART), bf16),
            v((HIST, HIST, ROWS, QUART), bf16),
            v((HIST, ROWS, QUART), bf16),
            v((HIST, ROWS, QUART), bf16),
            v((HIST, ROWS, QUART), bf16),
            v((ENT, SHARD, QUART), f32),
            v((ENT // CORES, SHARD, QUART), f32),
            v((XS, ZS, SHARD, QUART), bf16),
            v((XS, ZS, SHARD, QUART), bf16),
            v((ZS, SHARD, QUART), f32),
            v((ZS, SHARD, QUART), f32),
            v((8, QUART), f32),
            v((8, QUART), f32),
            dma((16,)),
            dma((2,)),
            dma((2, HIST)),
            dma((3, HIST)),
            dma((2, HIST)),
            dma((2, HIST)),
            dma((2, HIST)),
            dma((2, HIST)),
            dma((2, HIST)),
            dma((2,)),
            dma((2,)),
            dma((2, XS)),
            dma((2, ZS)),
            dma((2,)),
            dma((2, HIST)),
            dma((2, ZS)),
            dma((2, XS)),
            dma((2,)),
        ],
        compiler_params=pltpu.CompilerParams(
            collective_id=0, has_side_effects=True, vmem_limit_bytes=50 << 20
        ),
        name="encoder_backward",
    )(
        states,
        w_neigh,
        w_self,
        w_gate,
        b_gate.reshape(1, D),
        relation,
        edge_src,
        edge_rel,
        edge_dst,
        send_counts,
        query_ent.reshape(1, 128),
        query_rel.reshape(1, 128),
        query_grad,
    )
    result, grad_neigh, grad_self, grad_gate, grad_bias, grad_rel = pl.pallas_call(
        functools.partial(unfold, factor),
        out_shape=(
            shape((1, ROWS, D), f32),
            shape((2, HALF, HALF), f32),
            shape((D, D), f32),
            shape((D, D), f32),
            shape((1, D), f32),
            shape((NREL, D), f32),
        ),
        in_specs=[vmem] * 2,
        out_specs=(vmem,) * 6,
        compiler_params=pltpu.CompilerParams(vmem_limit_bytes=32 << 20),
        name="unfold",
    )(gathered, result)
    return result, grad_neigh, grad_self, grad_gate, grad_bias.reshape(D), grad_rel


def solution(mesh):
    return jax.shard_map(
        on_device,
        mesh=mesh,
        in_specs=(
            P("hist", "ent", None),
            P(),
            P(),
            P(),
            P(),
            P(),
            P("hist", "ent"),
            P("hist", "ent"),
            P("hist", "ent"),
            P("hist", "ent"),
            P("ent"),
            P("ent"),
            P("ent", None),
        ),
        out_specs=(P("hist", "ent", None), P(), P(), P(), P(), P()),
        check_vma=False,
    )
```

time: 157 us -> 135 us (0.86)
  Pallas kernels: 142 us -> 122 us
    pallas_call x1 -> x2, Pallas kernels: 142 us -> 122 us  [the longest x1 119 us: on_device(): pl.pallas_call(kernel, out_shape=(shape((ENT, HIST, KEPT, QUART), bf16),...]
    unnamed x38 -> x28, local copies, waits for them, and re-layouts: 13.7 us -> 12.2 us
where the time goes in v2:
time: 135 us; the launch traced here: 134 us
  Pallas kernels  122 us (90%)
  local copies, waits for them, and re-layouts  12.2 us (9%)
    pallas_call x1, Pallas kernels, on_device(): pl.pallas_call(kernel, out_shape=(shape((ENT, HIST, KEPT, QUART), bf16),...  119 us
    unnamed x28, local copies, waits for them, and re-layouts  12.2 us

profile of v2, /device:TPU:1, one launch (start us, length us, event | category | flops | bytes accessed | tf_op | source)
XLA Modules:
  0.0 134.5 jit_solution(16536369958126020352)
XLA Ops:
  0.6 0.0 copy-start.1
  0.6 1.0 copy-done.1
  1.7 0.0 copy-start.2
  1.7 1.0 copy-done.2
  2.7 0.0 copy-start.3
  2.7 1.0 copy-done.3
  3.7 0.0 copy-start.4
  3.7 0.9 copy-done.4
  4.7 0.0 copy-start.5
  4.7 0.9 copy-done.5
  5.6 0.0 copy-start.6
  5.7 0.9 copy-done.6
  6.6 0.0 copy-start.7
  6.6 0.7 copy-done.7
  7.3 0.7 copy-done.8
  8.0 0.7 copy-done.9
  8.6 0.7 copy-done.10
  9.3 0.7 copy-done.11
  10.0 0.7 copy-done.12
  10.6 0.7 copy-done.13
  11.3 119.2 %encoder_backward.1 = (bf16[64,4,32,128]{3,2,1,0:T(8,128)(2,1)}, bf16[4,256,128]{2,1,0:T(8,128)(2,1)S(1)}) custom-call(bf16[1,256,512]{2,1,0:T(8,128)(2,1)S(1)} %copy-done.4, bf16[2,256,256]{2,1,0:T(8,128)(2,1)S(1)} %copy-done.5, bf16[512,512]{1,0:T(8,128)(2,1)S(1)} %copy-done.1, bf16[512,512]{1,0:T(8,128)(2,1)S(1)} %copy-done.2, f32[1,512]{1,0:T(1,128)S(1)} %bitcast.4, ...), custom_call_target="tpu_custom_call" | custom-call | tf_op jit(solution)/shard_map/encoder_backward/pallas_call | solution.py:581
  130.5 0.0 copy-start
  130.5 1.6 %copy-done = bf16[64,4,32,128]{3,2,1,0:T(8,128)(2,1)S(1)} copy-done((bf16[64,4,32,128]{3,2,1,0:T(8,128)(2,1)S(1)}, bf16[64,4,32,128]{3,2,1,0:T(8,128)(2,1)}, u32[]{:S(2)}) %copy-start) | copy-done | bytes 2097176
  132.1 2.4 %unfold.1 = (f32[1,256,512]{2,1,0:T(8,128)}, f32[2,256,256]{2,1,0:T(8,128)}, f32[512,512]{1,0:T(8,128)}, f32[512,512]{1,0:T(8,128)}, f32[1,512]{1,0:T(1,128)}, /*index=5*/f32[460,512]{1,0:T(8,128)}) custom-call(bf16[64,4,32,128]{3,2,1,0:T(8,128)(2,1)S(1)} %copy-done, bf16[4,256,128]{2,1,0:T(8,128)(2,1)S(1)} %get-tuple-element.15.result), custom_call_target="tpu_custom_call" | custom-call | tf_op jit(solution)/shard_map/unfold/pallas_call | solution.py:673
  (6 shorter events, 0.0 us)
Async XLA Ops:
  0.6 1.0 copy-start.1
  1.7 1.0 copy-start.2
  2.7 1.0 copy-start.3
  3.7 0.9 copy-start.4
  4.7 0.9 copy-start.5
  5.6 0.9 copy-start.6
  6.6 0.7 copy-start.7
  7.3 0.7 copy-start.8
  8.0 0.7 copy-start.9
  8.6 0.7 copy-start.10
  9.3 0.7 copy-start.11
  10.0 0.7 copy-start.12
  10.6 0.7 copy-start.13
  130.5 1.6 %copy-start = (bf16[64,4,32,128]{3,2,1,0:T(8,128)(2,1)S(1)}, bf16[64,4,32,128]{3,2,1,0:T(8,128)(2,1)}, u32[]{:S(2)}) copy-start(bf16[64,4,32,128]{3,2,1,0:T(8,128)(2,1)} %get-tuple-element.14.gathered) | copy-start | bytes 6291460

commit v3 on v2

--- a/solution.py
+++ b/solution.py
@@ -22,10 +22,11 @@
 SLOTS = 512
 NREL = 460
 REL_PAD = 512
-R_GATE, R_SELF, R_NEIGH, R_REL, R_QUERY = 0, 8, 16, 24, 32
-SHARD = 40
-KEPT = 32
+R_GATE, R_SELF, R_QUERY, ROWS1 = 0, 8, 16, 24
+R_NEIGH, R_REL, ROWS2 = 0, 8, 16
+KEPT = 16
 BIAS_ROW = 508
+GROUP = ENT // CORES
 
 
 def nn(a, b):
@@ -85,7 +86,8 @@
     query_ent_in,
     query_rel_in,
     query_grad_in,
-    gathered,
+    gathered1,
+    gathered2,
     result,
     states,
     w_cols,
@@ -124,14 +126,22 @@
     sum_send,
     sum_recv,
     res_send,
-    grads,
-    core_recv,
-    x_send,
-    x_recv,
-    z_send,
-    z_recv,
-    rel_send,
-    rel_recv,
+    w_neigh,
+    grads1,
+    core_recv1,
+    sum1,
+    x_send1,
+    x_recv1,
+    z_send1,
+    z_recv1,
+    grads2,
+    core_recv2,
+    sum2,
+    x_send2,
+    x_recv2,
+    z_send2,
+    z_recv2,
+    y_recv2,
     fetch_sem,
     id_sem,
     fwd_id_sem,
@@ -143,13 +153,18 @@
     sum_sem,
     res_sem,
     core_sem,
-    x_sem,
-    z_sem,
-    rel_sem,
-    gy_sem,
-    gz_sem,
-    gx_sem,
-    gc_sem,
+    x1_sem,
+    z1_sem,
+    x2_sem,
+    z2_sem,
+    y2_sem,
+    gx1_sem,
+    gz1_sem,
+    gy1_sem,
+    gc1_sem,
+    gz2_sem,
+    gx2_sem,
+    gc2_sem,
 ):
     hist = lax.axis_index("hist")
     me = lax.axis_index("ent")
@@ -195,6 +210,7 @@
     fetch(query_ent_in, query_ent)
     fetch(query_rel_in, query_rel)
     fetch(query_grad_in.at[:, cols], query_grad)
+    fetch(w_neigh_in, w_neigh)
 
     lax.fori_loop(1, ENT, greet, 0)
     for i in range(1, HIST):
@@ -288,10 +304,12 @@
     hot_query = hot(iota((ROWS, 128), 0) == query_ent[...])
     cot[...] = nn(hot_query, q_parts[0]) + (nn(hot_query, q_parts[1]) + nn(hot_query, q_parts[2]))
     hot_query = hot(iota((REL_PAD, 128), 0) == query_rel[...])
-    grads[:, R_QUERY : R_QUERY + 8, :] = by_shard(
-        nn(hot_query, q_parts[0]) + (nn(hot_query, q_parts[1]) + nn(hot_query, q_parts[2]))
-    )
-    grads[32:, R_NEIGH : R_NEIGH + 8, :] = jnp.zeros((32, 8, QUART), f32)
+    by_query = nn(hot_query, q_parts[0]) + (nn(hot_query, q_parts[1]) + nn(hot_query, q_parts[2]))
+    for g in range(ENT):
+        c, xx, zz = g // GROUP, g // ZS % XS, g % ZS
+        at = c * GROUP + zz * XS + xx
+        grads1[at, R_QUERY : R_QUERY + 8, :] = by_query[g * 8 : (g + 1) * 8, :]
+    grads2[GROUP:, R_NEIGH : R_NEIGH + 8, :] = jnp.zeros((GROUP, 8, QUART), f32)
 
     def forward_messages(t):
         @pl.when(hist != t)
@@ -356,16 +374,51 @@
         share_states(t)
     forward_rest(top)
 
-    def add_grads(at, value, t, shards=ENT):
+    def add_grads(ref, at, value, t, owners=ENT):
         if t == top:
-            grads[:shards, at : at + 8, :] = by_shard(value)
+            ref[:owners, at : at + 8, :] = by_shard(value)
         else:
-            grads[:shards, at : at + 8, :] += by_shard(value)
+            ref[:owners, at : at + 8, :] += by_shard(value)
 
     def returned_grads(t):
         back = unpack(b_recv[t])
-        add_grads(R_NEIGH, tn(inputs[t], back), t, 32)
-        add_grads(R_REL, nn(hot_rel_t[t], back), t)
+        add_grads(grads2, R_NEIGH, tn(inputs[t], back), t, GROUP)
+        add_grads(grads2, R_REL, nn(hot_rel_t[t], back), t)
+
+    partner = me + 1 - 2 * core
+    mine = pl.multiple_of(core * GROUP, GROUP)
+    half = pl.ds(mine, GROUP)
+    other_half = pl.ds(pl.multiple_of((1 - core) * GROUP, GROUP), GROUP)
+
+    def along_x(src, dst, sem):
+        copies = []
+        for i in range(1, XS):
+            there = lax.rem(x + i, XS)
+            where = {"ent": me + (there - x) * (CORES * ZS)}
+            copies.append(remote(src(there), dst, sem.at[0, i], sem.at[1, i], where))
+        return copies
+
+    def along_z(src, dst, sem):
+        copies = []
+        for i in range(1, ZS):
+            there = lax.rem(z + i, ZS)
+            where = {"ent": me + (there - z) * CORES}
+            copies.append(remote(src(there), dst, sem.at[0, i], sem.at[1, i], where))
+        return copies
+
+    def along_hist(src, dst, sem):
+        copies = []
+        for i in range(1, HIST):
+            where = {"hist": lax.rem(hist + i, HIST)}
+            copies.append(remote(src, dst, sem.at[0, i], sem.at[1, i], where))
+        return copies
+
+    def to_core(src, dst, sem, i):
+        return remote(src, dst, sem.at[0, i], sem.at[1, i], {"ent": partner})
+
+    def finish(copies):
+        for copy in copies:
+            copy.wait()
 
     for t in range(top, -1, -1):
         c = cot[...]
@@ -394,11 +447,21 @@
         down = jnp.sum(gate_term, axis=0, keepdims=True)
         bias[...] = down if t == top else bias[...] + down
         for at, low in ((R_GATE, gate_low), (R_SELF, pre_low)):
-            add_grads(
-                at, jnp.concatenate([tn(states[t, 0], low), tn(states[t, 1], low)], axis=0), t
-            )
+            total = jnp.concatenate([tn(states[t, 0], low), tn(states[t, 1], low)], axis=0)
+            add_grads(grads1, at, total, t)
+        if t == 0:
+            row = R_QUERY + BIAS_ROW % 8
+            grads1[BIAS_ROW // 8, row : row + 1, :] = bias[...]
+            core1 = to_core(grads1.at[other_half], core_recv1, core_sem, 0)
         if t < top:
             returned_grads(t + 1)
+        if t == 0:
+            core1.wait()
+            both = (grads1[half] + core_recv1[...]).reshape(ZS, XS, ROWS1, QUART)
+            sum1[...] = both
+            for xx in range(XS):
+                x_send1[xx] = both[:, xx].astype(bf16)
+            x1 = along_x(lambda there: x_send1.at[there], x_recv1.at[x], x1_sem)
 
         wait_bytes(b_recv.at[t, others], b_sem.at[1, t])
         high, low = split(nn(hot_src_t[t], unpack(b_recv[t])))
@@ -409,6 +472,15 @@
         near_part = nt(high, w_own[...]) + nt(low, w_own[...]) + c * keep[t] + part[hist]
         if t > 0:
             forward_rest(t - 1)
+        else:
+            returned_grads(0)
+            core2 = to_core(grads2.at[other_half], core_recv2, core_sem, 1)
+            finish(x1)
+            total = sum1[:, x]
+            for i in range(1, XS):
+                total = total + x_recv1[lax.rem(x + i, XS)].astype(f32)
+            z_send1[...] = total
+            z1 = along_z(lambda there: z_send1.at[there], z_recv1.at[z], z1_sem)
         wait_bytes(part_recv.at[t, pl.ds(0, HIST - 1)], part_sem.at[1, t])
         for i in range(1, HIST):
             near_part = near_part + part_recv[t, lax.rem(hist + i, HIST)].astype(f32)
@@ -431,101 +503,75 @@
                 {"hist": t},
             )
 
-    returned_grads(0)
-    grads[BIAS_ROW // 8, R_QUERY + BIAS_ROW % 8 : R_QUERY + BIAS_ROW % 8 + 1, :] = bias[...]
-
-    partner = me + 1 - 2 * core
-    half = ENT // CORES
-    mine = pl.multiple_of(core * half, half)
-    remote(
-        grads.at[pl.ds(pl.multiple_of((1 - core) * half, half), half)],
-        core_recv,
-        core_sem.at[0],
-        core_sem.at[1],
-        {"ent": partner},
-    ).wait()
-    x_send[...] = (grads[pl.ds(mine, half)] + core_recv[...]).astype(bf16).reshape(
-        XS, ZS, SHARD, QUART
-    )
-    copies = []
+    core2.wait()
+    both = (grads2[half] + core_recv2[...]).reshape(XS, ZS, ROWS2, QUART)
+    sum2[...] = both
+    x_send2[...] = both.astype(bf16)
+    x2 = along_x(lambda there: x_send2.at[there], x_recv2.at[x], x2_sem)
+
+    finish(z1)
+    shard1 = z_send1[z]
+    for i in range(1, ZS):
+        shard1 = shard1 + z_recv1[lax.rem(z + i, ZS)]
+    place1 = mine + z * XS + x
+    gathered1[hist, place1] = shard1[:KEPT, :].astype(bf16)
+    own1 = gathered1.at[hist, place1]
+    gx1 = along_x(lambda there: own1, own1, gx1_sem)
+
+    finish(x2)
+    total = sum2[x]
     for i in range(1, XS):
-        there = lax.rem(x + i, XS)
-        copies.append(
-            remote(
-                x_send.at[there],
-                x_recv.at[x],
-                x_sem.at[0, i],
-                x_sem.at[1, i],
-                {"ent": me + (there - x) * (CORES * ZS)},
-            )
+        total = total + x_recv2[lax.rem(x + i, XS)].astype(f32)
+    z_send2[...] = total
+    z2 = along_z(lambda there: z_send2.at[there], z_recv2.at[z], z2_sem)
+
+    finish(gx1)
+    line1 = gathered1.at[hist, pl.ds(mine + z * XS, XS)]
+    gz1 = along_z(lambda there: line1, line1, gz1_sem)
+
+    finish(z2)
+    shard2 = z_send2[z]
+    for i in range(1, ZS):
+        shard2 = shard2 + z_recv2[lax.rem(z + i, ZS)]
+    y_recv2[hist] = jnp.concatenate([shard2, shard1[R_QUERY:, :]], axis=0)
+    y2 = along_hist(y_recv2.at[hist], y_recv2.at[hist], y2_sem)
+
+    finish(gz1)
+    plane1 = gathered1.at[hist, half]
+    last1 = [to_core(plane1, plane1, gc1_sem, 0)]
+    gy1 = along_hist(plane1, plane1, gy1_sem)
+
+    finish(y2)
+    place2 = mine + x * ZS + z
+    for b in range(2):
+        wide = jnp.concatenate(
+            [y_recv2[2 * b, R_REL : R_REL + 8, :], y_recv2[2 * b + 1, R_REL : R_REL + 8, :]], axis=1
         )
-    total = grads[pl.ds(mine + x * ZS, ZS)] + core_recv[pl.ds(x * ZS, ZS)]
-    for copy in copies:
-        copy.wait()
+        high = wide.astype(bf16).astype(f32)
+        twice = nt(jnp.concatenate([high, wide - high], axis=0).astype(bf16), w_neigh[b])
+        by_rel = twice[:8, :] + twice[8:, :]
+        for j in range(2):
+            h = 2 * b + j
+            rel_rows = by_rel[:, j * QUART : (j + 1) * QUART] + y_recv2[h, ROWS2:, :]
+            gathered2[place2, h] = jnp.concatenate(
+                [y_recv2[h, R_NEIGH : R_NEIGH + 8, :], rel_rows], axis=0
+            ).astype(bf16)
+    own2 = gathered2.at[place2]
+    gz2 = along_z(lambda there: own2, own2, gz2_sem)
+    finish(gz2)
+    line2 = gathered2.at[pl.ds(mine + x * ZS, ZS)]
+    gx2 = along_x(lambda there: line2, line2, gx2_sem)
+    last2 = [to_core(line2, line2, gc2_sem, 0)]
+    for i in range(1, HIST):
+        gy1[i - 1].wait()
+        came = gathered1.at[lax.rem(hist + HIST - i, HIST), half]
+        last1.append(to_core(came, came, gc1_sem, i))
     for i in range(1, XS):
-        total = total + x_recv[lax.rem(x + i, XS)].astype(f32)
-    z_send[...] = total
-    copies = []
-    for i in range(1, ZS):
-        there = lax.rem(z + i, ZS)
-        copies.append(
-            remote(
-                z_send.at[there],
-                z_recv.at[z],
-                z_sem.at[0, i],
-                z_sem.at[1, i],
-                {"ent": me + (there - z) * CORES},
-            )
-        )
-    shard = z_send[z]
-    for copy in copies:
-        copy.wait()
-    for i in range(1, ZS):
-        shard = shard + z_recv[lax.rem(z + i, ZS)]
-
-    rel_send[...] = shard[R_REL : R_REL + 8, :]
-    remote(rel_send, rel_recv, rel_sem.at[0], rel_sem.at[1], {"hist": mate}).wait()
-    by_rel = shard[R_QUERY : R_QUERY + 8, :]
-    for v, w in ((rel_send[...], w_own), (rel_recv[...], w_other)):
-        high = v.astype(bf16).astype(f32)
-        both = nt(jnp.concatenate([high, v - high], axis=0).astype(bf16), w[...])
-        by_rel = by_rel + (both[:8, :] + both[8:, :])
-
-    place = mine + x * ZS + z
-    gathered[place, hist] = jnp.concatenate([shard[:R_REL, :], by_rel], axis=0).astype(bf16)
-    own = gathered.at[place, hist]
-    copies = []
-    for i in range(1, HIST):
-        there = lax.rem(hist + i, HIST)
-        copies.append(remote(own, own, gy_sem.at[0, i], gy_sem.at[1, i], {"hist": there}))
-    for copy in copies:
-        copy.wait()
-    own = gathered.at[place]
-    copies = []
-    for i in range(1, ZS):
-        there = lax.rem(z + i, ZS)
-        copies.append(
-            remote(own, own, gz_sem.at[0, i], gz_sem.at[1, i], {"ent": me + (there - z) * CORES})
-        )
-    for copy in copies:
-        copy.wait()
-    own = gathered.at[pl.ds(mine + x * ZS, ZS)]
-    copies = []
-    for i in range(1, XS):
-        there = lax.rem(x + i, XS)
-        copies.append(
-            remote(
-                own,
-                own,
-                gx_sem.at[0, i],
-                gx_sem.at[1, i],
-                {"ent": me + (there - x) * (CORES * ZS)},
-            )
-        )
-    for copy in copies:
-        copy.wait()
-    own = gathered.at[pl.ds(mine, half)]
-    remote(own, own, gc_sem.at[0], gc_sem.at[1], {"ent": partner}).wait()
+        gx2[i - 1].wait()
+        came = gathered2.at[pl.ds(mine + lax.rem(x + XS - i, XS) * ZS, ZS)]
+        last2.append(to_core(came, came, gc2_sem, i))
+    finish(last1)
+    finish(last2)
 
     three = pl.ds(0, HIST - 1)
     wait_bytes(result.at[three], res_sem.at[1])
@@ -541,15 +587,27 @@
         wait_bytes(sum_send.at[t], sum_sem.at[0, t])
 
 
-def unfold(factor, gathered, result, out_states, out_neigh, out_self, out_gate, out_bias, out_rel):
+def unfold(
+    factor,
+    gathered1,
+    gathered2,
+    result,
+    out_states,
+    out_neigh,
+    out_self,
+    out_gate,
+    out_bias,
+    out_rel,
+):
     for h in range(HIST):
         lanes = slice(h * QUART, (h + 1) * QUART)
         out_states[0, :, lanes] = result[h].astype(f32)
-        rows = gathered[:, h].astype(f32) * factor
+        rows = gathered1[h].astype(f32) * factor
         out_gate[:, lanes] = rows[:, R_GATE : R_GATE + 8, :].reshape(D, QUART)
         out_self[:, lanes] = rows[:, R_SELF : R_SELF + 8, :].reshape(D, QUART)
+        rows = gathered2[:, h].astype(f32) * factor
         out_neigh[h // 2, :, (h % 2) * QUART : (h % 2 + 1) * QUART] = rows[
-            :32, R_NEIGH : R_NEIGH + 8, :
+            :GROUP, R_NEIGH : R_NEIGH + 8, :
         ].reshape(HALF, QUART)
         by_rel = rows[:, R_REL : R_REL + 8, :].reshape(REL_PAD, QUART)
         out_rel[:, lanes] = by_rel[:NREL, :]
@@ -578,14 +636,15 @@
     shape = jax.ShapeDtypeStruct
     v = pltpu.VMEM
     i32 = jnp.int32
-    gathered, result = pl.pallas_call(
+    gathered1, gathered2, result = pl.pallas_call(
         kernel,
         out_shape=(
+            shape((HIST, ENT, KEPT, QUART), bf16),
             shape((ENT, HIST, KEPT, QUART), bf16),
             shape((HIST, ROWS, QUART), bf16),
         ),
         in_specs=[anywhere] * 13,
-        out_specs=(vmem,) * 2,
+        out_specs=(vmem,) * 3,
         scratch_shapes=[
             v((HIST, 2, ROWS, HALF), bf16),
             v((HALF, QUART), bf16),
@@ -624,15 +683,23 @@
             v((HIST, ROWS, QUART), bf16),
             v((HIST, ROWS, QUART), bf16),
             v((HIST, ROWS, QUART), bf16),
-            v((ENT, SHARD, QUART), f32),
-            v((ENT // CORES, SHARD, QUART), f32),
-            v((XS, ZS, SHARD, QUART), bf16),
-            v((XS, ZS, SHARD, QUART), bf16),
-            v((ZS, SHARD, QUART), f32),
-            v((ZS, SHARD, QUART), f32),
-            v((8, QUART), f32),
-            v((8, QUART), f32),
-            dma((16,)),
+            v((2, HALF, HALF), bf16),
+            v((ENT, ROWS1, QUART), f32),
+            v((GROUP, ROWS1, QUART), f32),
+            v((ZS, XS, ROWS1, QUART), f32),
+            v((XS, ZS, ROWS1, QUART), bf16),
+            v((XS, ZS, ROWS1, QUART), bf16),
+            v((ZS, ROWS1, QUART), f32),
+            v((ZS, ROWS1, QUART), f32),
+            v((ENT, ROWS2, QUART), f32),
+            v((GROUP, ROWS2, QUART), f32),
+            v((XS, ZS, ROWS2, QUART), f32),
+            v((XS, ZS, ROWS2, QUART), bf16),
+            v((XS, ZS, ROWS2, QUART), bf16),
+            v((ZS, ROWS2, QUART), f32),
+            v((ZS, ROWS2, QUART), f32),
+            v((HIST, ROWS2 + 8, QUART), f32),
+            dma((17,)),
             dma((2,)),
             dma((2, HIST)),
             dma((3, HIST)),
@@ -642,17 +709,22 @@
             dma((2, HIST)),
             dma((2, HIST)),
             dma((2,)),
-            dma((2,)),
+            dma((2, 2)),
             dma((2, XS)),
             dma((2, ZS)),
-            dma((2,)),
+            dma((2, XS)),
+            dma((2, ZS)),
+            dma((2, HIST)),
+            dma((2, XS)),
+            dma((2, ZS)),
+            dma((2, HIST)),
             dma((2, HIST)),
             dma((2, ZS)),
             dma((2, XS)),
-            dma((2,)),
+            dma((2, XS)),
         ],
         compiler_params=pltpu.CompilerParams(
-            collective_id=0, has_side_effects=True, vmem_limit_bytes=50 << 20
+            collective_id=0, has_side_effects=True, vmem_limit_bytes=54 << 20
         ),
         name="encoder_backward",
     )(
@@ -680,11 +752,11 @@
             shape((1, D), f32),
             shape((NREL, D), f32),
         ),
-        in_specs=[vmem] * 2,
+        in_specs=[vmem] * 3,
         out_specs=(vmem,) * 6,
         compiler_params=pltpu.CompilerParams(vmem_limit_bytes=32 << 20),
         name="unfold",
-    )(gathered, result)
+    )(gathered1, gathered2, result)
     return result, grad_neigh, grad_self, grad_gate, grad_bias.reshape(D), grad_rel
 
 

time: 135 us -> 112 us (0.83)
  Pallas kernels: 122 us -> 108 us
  local copies, waits for them, and re-layouts: 12.2 us -> 3.39 us
    pallas_call x1, Pallas kernels: 119 us -> 106 us  [on_device(): pl.pallas_call(kernel, out_shape=(shape((HIST, ENT, KEPT, QUART), bf16),...]
    unnamed x28 -> x6, local copies, waits for them, and re-layouts: 12.2 us -> 3.39 us
where the time goes in v3:
time: 112 us
  Pallas kernels  108 us (96%)
  local copies, waits for them, and re-layouts  3.39 us (3%)
    pallas_call x1, Pallas kernels, on_device(): pl.pallas_call(kernel, out_shape=(shape((HIST, ENT, KEPT, QUART), bf16),...  106 us
    unnamed x6, local copies, waits for them, and re-layouts  3.39 us
    pallas_call x1, Pallas kernels, on_device(): pl.pallas_call(functools.partial(unfold, factor), out_shape=(shape((1, RO...  2.36 us

profile of v3, /device:TPU:1, one launch (start us, length us, event | category | flops | bytes accessed | tf_op | source)
XLA Modules:
  0.0 112.0 jit_solution(9888854657268470481)
XLA Ops:
  0.6 105.6 %encoder_backward.1 = (bf16[4,64,16,128]{3,2,1,0:T(8,128)(2,1)}, bf16[64,4,16,128]{3,2,1,0:T(8,128)(2,1)}, bf16[4,256,128]{2,1,0:T(8,128)(2,1)}) custom-call(bf16[1,256,512]{2,1,0:T(8,128)(2,1)} %states_in.1, bf16[2,256,256]{2,1,0:T(8,128)(2,1)} %w_neigh_in.1, bf16[512,512]{1,0:T(8,128)(2,1)} %w_self_in.1, bf16[512,512]{1,0:T(8,128)(2,1)} %w_gate_in.1, ...), custom_call_target="tpu_custom_call" | custom-call | tf_op jit(solution)/shard_map/encoder_backward/pallas_call | solution.py:639
  106.3 0.0 copy-start
  106.3 1.2 %copy-done = bf16[4,64,16,128]{3,2,1,0:T(8,128)(2,1)S(1)} copy-done((bf16[4,64,16,128]{3,2,1,0:T(8,128)(2,1)S(1)}, bf16[4,64,16,128]{3,2,1,0:T(8,128)(2,1)}, u32[]{:S(2)}) %copy-start) | copy-done | bytes 1048600
  107.5 0.0 copy-start.1
  107.5 1.2 %copy-done.1 = bf16[64,4,16,128]{3,2,1,0:T(8,128)(2,1)S(1)} copy-done((bf16[64,4,16,128]{3,2,1,0:T(8,128)(2,1)S(1)}, bf16[64,4,16,128]{3,2,1,0:T(8,128)(2,1)}, u32[]{:S(2)}) %copy-start.1) | copy-done | bytes 1048600
  108.7 0.0 copy-start.2
  108.7 0.9 copy-done.2
  109.7 2.4 %unfold.1 = (f32[1,256,512]{2,1,0:T(8,128)}, f32[2,256,256]{2,1,0:T(8,128)}, f32[512,512]{1,0:T(8,128)}, f32[512,512]{1,0:T(8,128)}, f32[1,512]{1,0:T(1,128)}, /*index=5*/f32[460,512]{1,0:T(8,128)}) custom-call(bf16[4,64,16,128]{3,2,1,0:T(8,128)(2,1)S(1)} %copy-done, bf16[64,4,16,128]{3,2,1,0:T(8,128)(2,1)S(1)} %copy-done.1, bf16[4,256,128]{2,1,0:T(8,128)(2,1)S(1)} %copy-done.2), custom_call_target="tpu_custom_call" | custom-call | tf_op jit(solution)/shard_map/unfold/pallas_call | solution.py:745
Async XLA Ops:
  106.3 1.2 %copy-start = (bf16[4,64,16,128]{3,2,1,0:T(8,128)(2,1)S(1)}, bf16[4,64,16,128]{3,2,1,0:T(8,128)(2,1)}, u32[]{:S(2)}) copy-start(bf16[4,64,16,128]{3,2,1,0:T(8,128)(2,1)} %get-tuple-element.15.gathered1) | copy-start | bytes 3145732
  107.5 1.2 %copy-start.1 = (bf16[64,4,16,128]{3,2,1,0:T(8,128)(2,1)S(1)}, bf16[64,4,16,128]{3,2,1,0:T(8,128)(2,1)}, u32[]{:S(2)}) copy-start(bf16[64,4,16,128]{3,2,1,0:T(8,128)(2,1)} %get-tuple-element.16.gathered2) | copy-start | bytes 3145732
  108.7 0.9 copy-start.2

commit v4 on v3

--- a/solution.py
+++ b/solution.py
@@ -88,6 +88,7 @@
     query_grad_in,
     gathered1,
     gathered2,
+    gathered3,
     result,
     states,
     w_cols,
@@ -165,6 +166,10 @@
     gz2_sem,
     gx2_sem,
     gc2_sem,
+    gx3_sem,
+    gz3_sem,
+    gy3_sem,
+    gc3_sem,
 ):
     hist = lax.axis_index("hist")
     me = lax.axis_index("ent")
@@ -183,6 +188,12 @@
             barrier, inc=1, device_id={"ent": lax.rem(me + i, ENT)}, device_id_type=MESH
         )
         return carry
+
+    lax.fori_loop(1, ENT, greet, 0)
+    for i in range(1, HIST):
+        pl.semaphore_signal(
+            barrier, inc=1, device_id={"hist": lax.rem(hist + i, HIST)}, device_id_type=MESH
+        )
 
     cols = pl.ds(pl.multiple_of(hist * QUART, QUART), QUART)
     near = pl.ds(pl.multiple_of(side * QUART, QUART), QUART)
@@ -211,12 +222,6 @@
     fetch(query_rel_in, query_rel)
     fetch(query_grad_in.at[:, cols], query_grad)
     fetch(w_neigh_in, w_neigh)
-
-    lax.fori_loop(1, ENT, greet, 0)
-    for i in range(1, HIST):
-        pl.semaphore_signal(
-            barrier, inc=1, device_id={"hist": lax.rem(hist + i, HIST)}, device_id_type=MESH
-        )
 
     fetched[0].wait()
     fetched[1].wait()
@@ -318,7 +323,8 @@
             wait_bytes(states.at[t, block], st_sem.at[1 + block, t])
 
         if t == top:
-            share_states(t - 1)
+            for later in range(t - 1, -1, -1):
+                share_states(later)
         hot_src_t[t] = hot(iota((ROWS, SLOTS), 0) == ids[t, 0:1, :])
         hot_rel_t[t] = hot(iota((REL_PAD, SLOTS), 0) == ids[t, 1:2, :])
         inputs[t] = (
@@ -370,8 +376,6 @@
             fwd_id_sem.at[1, hist],
             {"hist": lax.rem(hist + i, HIST)},
         )
-    for t in range(top - 1):
-        share_states(t)
     forward_rest(top)
 
     def add_grads(ref, at, value, t, owners=ENT):
@@ -442,13 +446,16 @@
                 part_sem.at[1, t],
                 {"hist": there},
             )
-        if t > 0:
+        if t == top:
             forward_messages(t - 1)
+        if t > 1:
+            forward_messages(t - 2)
         down = jnp.sum(gate_term, axis=0, keepdims=True)
         bias[...] = down if t == top else bias[...] + down
-        for at, low in ((R_GATE, gate_low), (R_SELF, pre_low)):
-            total = jnp.concatenate([tn(states[t, 0], low), tn(states[t, 1], low)], axis=0)
-            add_grads(grads1, at, total, t)
+        lows = jnp.concatenate([gate_low, pre_low], axis=1)
+        total = jnp.concatenate([tn(states[t, 0], lows), tn(states[t, 1], lows)], axis=0)
+        add_grads(grads1, R_GATE, total[:, :QUART], t)
+        add_grads(grads1, R_SELF, total[:, QUART:], t)
         if t == 0:
             row = R_QUERY + BIAS_ROW % 8
             grads1[BIAS_ROW // 8, row : row + 1, :] = bias[...]
@@ -463,6 +470,8 @@
                 x_send1[xx] = both[:, xx].astype(bf16)
             x1 = along_x(lambda there: x_send1.at[there], x_recv1.at[x], x1_sem)
 
+        if 0 < t < top:
+            forward_rest(t - 1)
         wait_bytes(b_recv.at[t, others], b_sem.at[1, t])
         high, low = split(nn(hot_src_t[t], unpack(b_recv[t])))
         sum_send[t] = high
@@ -470,9 +479,9 @@
             sum_send.at[t], sum_recv.at[t], sum_sem.at[0, t], sum_sem.at[1, t], {"hist": mate}
         )
         near_part = nt(high, w_own[...]) + nt(low, w_own[...]) + c * keep[t] + part[hist]
-        if t > 0:
+        if t == top:
             forward_rest(t - 1)
-        else:
+        if t == 0:
             returned_grads(0)
             core2 = to_core(grads2.at[other_half], core_recv2, core_sem, 1)
             finish(x1)
@@ -533,45 +542,54 @@
     shard2 = z_send2[z]
     for i in range(1, ZS):
         shard2 = shard2 + z_recv2[lax.rem(z + i, ZS)]
-    y_recv2[hist] = jnp.concatenate([shard2, shard1[R_QUERY:, :]], axis=0)
+    y_recv2[hist] = jnp.concatenate([shard2[R_REL:, :], shard1[R_QUERY:, :]], axis=0)
     y2 = along_hist(y_recv2.at[hist], y_recv2.at[hist], y2_sem)
+    gathered3[hist, place1] = shard2[:R_REL, :].astype(bf16)
+    own3 = gathered3.at[hist, place1]
+    gx3 = along_x(lambda there: own3, own3, gx3_sem)
 
     finish(gz1)
     plane1 = gathered1.at[hist, half]
-    last1 = [to_core(plane1, plane1, gc1_sem, 0)]
+    last = [to_core(plane1, plane1, gc1_sem, 0)]
     gy1 = along_hist(plane1, plane1, gy1_sem)
 
     finish(y2)
     place2 = mine + x * ZS + z
     for b in range(2):
-        wide = jnp.concatenate(
-            [y_recv2[2 * b, R_REL : R_REL + 8, :], y_recv2[2 * b + 1, R_REL : R_REL + 8, :]], axis=1
-        )
+        wide = jnp.concatenate([y_recv2[2 * b, :8, :], y_recv2[2 * b + 1, :8, :]], axis=1)
         high = wide.astype(bf16).astype(f32)
         twice = nt(jnp.concatenate([high, wide - high], axis=0).astype(bf16), w_neigh[b])
         by_rel = twice[:8, :] + twice[8:, :]
         for j in range(2):
             h = 2 * b + j
-            rel_rows = by_rel[:, j * QUART : (j + 1) * QUART] + y_recv2[h, ROWS2:, :]
-            gathered2[place2, h] = jnp.concatenate(
-                [y_recv2[h, R_NEIGH : R_NEIGH + 8, :], rel_rows], axis=0
-            ).astype(bf16)
+            rel_rows = by_rel[:, j * QUART : (j + 1) * QUART] + y_recv2[h, 8:, :]
+            gathered2[place2, h] = rel_rows.astype(bf16)
     own2 = gathered2.at[place2]
     gz2 = along_z(lambda there: own2, own2, gz2_sem)
+    finish(gx3)
+    line3 = gathered3.at[hist, pl.ds(mine + z * XS, XS)]
+    gz3 = along_z(lambda there: line3, line3, gz3_sem)
     finish(gz2)
     line2 = gathered2.at[pl.ds(mine + x * ZS, ZS)]
     gx2 = along_x(lambda there: line2, line2, gx2_sem)
-    last2 = [to_core(line2, line2, gc2_sem, 0)]
+    last.append(to_core(line2, line2, gc2_sem, 0))
+    finish(gz3)
+    plane3 = gathered3.at[hist, half]
+    gy3 = along_hist(plane3, plane3, gy3_sem)
+    last.append(to_core(plane3, plane3, gc3_sem, 0))
     for i in range(1, HIST):
         gy1[i - 1].wait()
         came = gathered1.at[lax.rem(hist + HIST - i, HIST), half]
-        last1.append(to_core(came, came, gc1_sem, i))
+        last.append(to_core(came, came, gc1_sem, i))
     for i in range(1, XS):
         gx2[i - 1].wait()
         came = gathered2.at[pl.ds(mine + lax.rem(x + XS - i, XS) * ZS, ZS)]
-        last2.append(to_core(came, came, gc2_sem, i))
-    finish(last1)
-    finish(last2)
+        last.append(to_core(came, came, gc2_sem, i))
+    for i in range(1, HIST):
+        gy3[i - 1].wait()
+        came = gathered3.at[lax.rem(hist + HIST - i, HIST), half]
+        last.append(to_core(came, came, gc3_sem, i))
+    finish(last)
 
     three = pl.ds(0, HIST - 1)
     wait_bytes(result.at[three], res_sem.at[1])
@@ -589,29 +607,72 @@
 
 def unfold(
     factor,
-    gathered1,
-    gathered2,
-    result,
+    gathered1_in,
+    gathered2_in,
+    gathered3_in,
+    result_in,
     out_states,
     out_neigh,
     out_self,
     out_gate,
     out_bias,
     out_rel,
+    gathered1,
+    gathered2,
+    gathered3,
+    result,
+    new_states,
+    new_neigh,
+    new_self,
+    new_gate,
+    new_bias,
+    new_rel,
+    in_sem,
+    out_sem,
 ):
+    fetched = []
+    for src, dst in (
+        (gathered1_in, gathered1),
+        (result_in, result),
+        (gathered2_in, gathered2),
+        (gathered3_in, gathered3),
+    ):
+        fetched.append(pltpu.make_async_copy(src, dst, in_sem.at[len(fetched)]))
+        fetched[-1].start()
+    stored = []
+
+    def store(src, dst):
+        stored.append(pltpu.make_async_copy(src, dst, out_sem.at[len(stored)]))
+        stored[-1].start()
+
+    fetched[0].wait()
+    for at, new, out in ((R_GATE, new_gate, out_gate), (R_SELF, new_self, out_self)):
+        for h in range(HIST):
+            rows = gathered1[h].astype(f32)[:, at : at + 8, :] * factor
+            new[:, h * QUART : (h + 1) * QUART] = rows.reshape(D, QUART)
+        store(new, out)
+    fetched[1].wait()
+    for h in range(HIST):
+        new_states[0, :, h * QUART : (h + 1) * QUART] = result[h].astype(f32)
+    store(new_states, out_states)
+    fetched[2].wait()
     for h in range(HIST):
         lanes = slice(h * QUART, (h + 1) * QUART)
-        out_states[0, :, lanes] = result[h].astype(f32)
-        rows = gathered1[h].astype(f32) * factor
-        out_gate[:, lanes] = rows[:, R_GATE : R_GATE + 8, :].reshape(D, QUART)
-        out_self[:, lanes] = rows[:, R_SELF : R_SELF + 8, :].reshape(D, QUART)
-        rows = gathered2[:, h].astype(f32) * factor
-        out_neigh[h // 2, :, (h % 2) * QUART : (h % 2 + 1) * QUART] = rows[
-            :GROUP, R_NEIGH : R_NEIGH + 8, :
-        ].reshape(HALF, QUART)
-        by_rel = rows[:, R_REL : R_REL + 8, :].reshape(REL_PAD, QUART)
-        out_rel[:, lanes] = by_rel[:NREL, :]
-        out_bias[:, lanes] = by_rel[BIAS_ROW : BIAS_ROW + 1, :]
+        by_rel = (gathered2[:, h].astype(f32) * factor).reshape(REL_PAD, QUART)
+        new_rel[:, lanes] = by_rel[:NREL, :]
+        new_bias[:, lanes] = by_rel[BIAS_ROW : BIAS_ROW + 1, :]
+    store(new_rel, out_rel)
+    fetched[3].wait()
+    for h in range(HIST):
+        lanes = slice((h % 2) * QUART, (h % 2 + 1) * QUART)
+        rows = gathered3[h, :GROUP].astype(f32) * factor
+        for g in range(GROUP):
+            at = g % ZS * XS + g // ZS
+            new_neigh[h // 2, g * 8 : (g + 1) * 8, lanes] = rows[at]
+    store(new_neigh, out_neigh)
+    store(new_bias, out_bias)
+    for copy in stored:
+        copy.wait()
 
 
 def on_device(
@@ -636,15 +697,16 @@
     shape = jax.ShapeDtypeStruct
     v = pltpu.VMEM
     i32 = jnp.int32
-    gathered1, gathered2, result = pl.pallas_call(
+    gathered1, gathered2, gathered3, result = pl.pallas_call(
         kernel,
         out_shape=(
             shape((HIST, ENT, KEPT, QUART), bf16),
-            shape((ENT, HIST, KEPT, QUART), bf16),
+            shape((ENT, HIST, 8, QUART), bf16),
+            shape((HIST, ENT, 8, QUART), bf16),
             shape((HIST, ROWS, QUART), bf16),
         ),
         in_specs=[anywhere] * 13,
-        out_specs=(vmem,) * 3,
+        out_specs=(vmem,) * 4,
         scratch_shapes=[
             v((HIST, 2, ROWS, HALF), bf16),
             v((HALF, QUART), bf16),
@@ -698,7 +760,7 @@
             v((XS, ZS, ROWS2, QUART), bf16),
             v((ZS, ROWS2, QUART), f32),
             v((ZS, ROWS2, QUART), f32),
-            v((HIST, ROWS2 + 8, QUART), f32),
+            v((HIST, 16, QUART), f32),
             dma((17,)),
             dma((2,)),
             dma((2, HIST)),
@@ -722,6 +784,10 @@
             dma((2, ZS)),
             dma((2, XS)),
             dma((2, XS)),
+            dma((2, XS)),
+            dma((2, ZS)),
+            dma((2, HIST)),
+            dma((2, HIST)),
         ],
         compiler_params=pltpu.CompilerParams(
             collective_id=0, has_side_effects=True, vmem_limit_bytes=54 << 20
@@ -752,11 +818,25 @@
             shape((1, D), f32),
             shape((NREL, D), f32),
         ),
-        in_specs=[vmem] * 3,
-        out_specs=(vmem,) * 6,
-        compiler_params=pltpu.CompilerParams(vmem_limit_bytes=32 << 20),
+        in_specs=[anywhere] * 4,
+        out_specs=(anywhere,) * 6,
+        scratch_shapes=[
+            v((HIST, ENT, KEPT, QUART), bf16),
+            v((ENT, HIST, 8, QUART), bf16),
+            v((HIST, ENT, 8, QUART), bf16),
+            v((HIST, ROWS, QUART), bf16),
+            v((1, ROWS, D), f32),
+            v((2, HALF, HALF), f32),
+            v((D, D), f32),
+            v((D, D), f32),
+            v((1, D), f32),
+            v((NREL, D), f32),
+            dma((4,)),
+            dma((6,)),
+        ],
+        compiler_params=pltpu.CompilerParams(vmem_limit_bytes=54 << 20),
         name="unfold",
-    )(gathered1, gathered2, result)
+    )(gathered1, gathered2, gathered3, result)
     return result, grad_neigh, grad_self, grad_gate, grad_bias.reshape(D), grad_rel
 
 

time: 112 us -> 107 us (0.955)
  local copies, waits for them, and re-layouts: 3.39 us -> 0 us
  Pallas kernels: 108 us -> 106 us
    unnamed x6 -> x0, local copies, waits for them, and re-layouts: 3.39 us -> none
    pallas_call x1, Pallas kernels: 106 us -> 103 us  [on_device(): pl.pallas_call(kernel, out_shape=(shape((HIST, ENT, KEPT, QUART), bf16),...]
where the time goes in v4:
time: 107 us
  Pallas kernels  106 us (99%)
    pallas_call x1, Pallas kernels, on_device(): pl.pallas_call(kernel, out_shape=(shape((HIST, ENT, KEPT, QUART), bf16),...  103 us
    pallas_call x1, Pallas kernels, on_device(): pl.pallas_call(functools.partial(unfold, factor), out_shape=(shape((1, RO...  3.42 us

profile of v4, /device:TPU:1, one launch (start us, length us, event | category | flops | bytes accessed | tf_op | source)
XLA Modules:
  0.0 107.0 jit_solution(3890944295011245158)
XLA Ops:
  0.6 102.9 %encoder_backward.1 = (bf16[4,64,16,128]{3,2,1,0:T(8,128)(2,1)}, bf16[64,4,8,128]{3,2,1,0:T(8,128)(2,1)}, bf16[4,64,8,128]{3,2,1,0:T(8,128)(2,1)}, bf16[4,256,128]{2,1,0:T(8,128)(2,1)}) custom-call(bf16[1,256,512]{2,1,0:T(8,128)(2,1)} %states_in.1, bf16[2,256,256]{2,1,0:T(8,128)(2,1)} %w_neigh_in.1, bf16[512,512]{1,0:T(8,128)(2,1)} %w_self_in.1, ...), custom_call_target="tpu_custom_call" | custom-call | tf_op jit(solution)/shard_map/encoder_backward/pallas_call | solution.py:700
  103.6 3.4 %unfold.1 = (f32[1,256,512]{2,1,0:T(8,128)}, f32[2,256,256]{2,1,0:T(8,128)}, f32[512,512]{1,0:T(8,128)}, f32[512,512]{1,0:T(8,128)}, f32[1,512]{1,0:T(1,128)}, /*index=5*/f32[460,512]{1,0:T(8,128)}) custom-call(bf16[4,64,16,128]{3,2,1,0:T(8,128)(2,1)} %get-tuple-element.16.gathered1_in, bf16[64,4,8,128]{3,2,1,0:T(8,128)(2,1)} %get-tuple-element.17.gathered2_in, ...), custom_call_target="tpu_custom_call" | custom-call | tf_op jit(solution)/shard_map/unfold/pallas_call | solution.py:811

commit v5 on v4

--- a/solution.py
+++ b/solution.py
@@ -424,6 +424,17 @@
         for copy in copies:
             copy.wait()
 
+    def send_result(t):
+        @pl.when(hist != t)
+        def _():
+            remote(
+                res_send.at[t],
+                result.at[hist],
+                res_sem.at[0],
+                res_sem.at[1],
+                {"hist": t},
+            )
+
     for t in range(top, -1, -1):
         c = cot[...]
         pre_term = c * coef_pre[t]
@@ -478,6 +489,8 @@
         remote(
             sum_send.at[t], sum_recv.at[t], sum_sem.at[0, t], sum_sem.at[1, t], {"hist": mate}
         )
+        if t < top:
+            send_result(t + 1)
         near_part = nt(high, w_own[...]) + nt(low, w_own[...]) + c * keep[t] + part[hist]
         if t == top:
             forward_rest(t - 1)
@@ -502,15 +515,8 @@
         def _():
             result[t] = res_send[t]
 
-        @pl.when(hist != t)
-        def _():
-            remote(
-                res_send.at[t],
-                result.at[hist],
-                res_sem.at[0],
-                res_sem.at[1],
-                {"hist": t},
-            )
+        if t == 0:
+            send_result(t)
 
     core2.wait()
     both = (grads2[half] + core_recv2[...]).reshape(XS, ZS, ROWS2, QUART)

time: 107 us -> 108 us (level)
  no operation moved by 1% of the time
where the time goes in v5:
time: 108 us
  Pallas kernels  107 us (99%)
    pallas_call x1, Pallas kernels, on_device(): pl.pallas_call(kernel, out_shape=(shape((HIST, ENT, KEPT, QUART), bf16),...  104 us
    pallas_call x1, Pallas kernels, on_device(): pl.pallas_call(functools.partial(unfold, factor), out_shape=(shape((1, RO...  3.42 us

profile of v5, /device:TPU:1, one launch (start us, length us, event | category | flops | bytes accessed | tf_op | source)
XLA Modules:
  0.0 107.7 jit_solution(16904225620823918898)
XLA Ops:
  0.6 103.6 %encoder_backward.1 = (bf16[4,64,16,128]{3,2,1,0:T(8,128)(2,1)}, bf16[64,4,8,128]{3,2,1,0:T(8,128)(2,1)}, bf16[4,64,8,128]{3,2,1,0:T(8,128)(2,1)}, bf16[4,256,128]{2,1,0:T(8,128)(2,1)}) custom-call(bf16[1,256,512]{2,1,0:T(8,128)(2,1)} %states_in.1, bf16[2,256,256]{2,1,0:T(8,128)(2,1)} %w_neigh_in.1, bf16[512,512]{1,0:T(8,128)(2,1)} %w_self_in.1, ...), custom_call_target="tpu_custom_call" | custom-call | tf_op jit(solution)/shard_map/encoder_backward/pallas_call | solution.py:706
  104.3 3.4 %unfold.1 = (f32[1,256,512]{2,1,0:T(8,128)}, f32[2,256,256]{2,1,0:T(8,128)}, f32[512,512]{1,0:T(8,128)}, f32[512,512]{1,0:T(8,128)}, f32[1,512]{1,0:T(1,128)}, /*index=5*/f32[460,512]{1,0:T(8,128)}) custom-call(bf16[4,64,16,128]{3,2,1,0:T(8,128)(2,1)} %get-tuple-element.16.gathered1_in, bf16[64,4,8,128]{3,2,1,0:T(8,128)(2,1)} %get-tuple-element.17.gathered2_in, ...), custom_call_target="tpu_custom_call" | custom-call | tf_op jit(solution)/shard_map/unfold/pallas_call | solution.py:817

commit v6 on v4

--- a/solution.py
+++ b/solution.py
@@ -24,7 +24,7 @@
 REL_PAD = 512
 R_GATE, R_SELF, R_QUERY, ROWS1 = 0, 8, 16, 24
 R_NEIGH, R_REL, ROWS2 = 0, 8, 16
-KEPT = 16
+KEPT = 8
 BIAS_ROW = 508
 GROUP = ENT // CORES
 
@@ -89,6 +89,7 @@
     gathered1,
     gathered2,
     gathered3,
+    gathered4,
     result,
     states,
     w_cols,
@@ -170,6 +171,10 @@
     gz3_sem,
     gy3_sem,
     gc3_sem,
+    gy4_sem,
+    gz4_sem,
+    gx4_sem,
+    gc4_sem,
 ):
     hist = lax.axis_index("hist")
     me = lax.axis_index("ent")
@@ -526,6 +531,10 @@
     gathered1[hist, place1] = shard1[:KEPT, :].astype(bf16)
     own1 = gathered1.at[hist, place1]
     gx1 = along_x(lambda there: own1, own1, gx1_sem)
+    place2 = mine + x * ZS + z
+    gathered4[place2, hist] = shard1[R_SELF : R_SELF + 8, :].astype(bf16)
+    own4 = gathered4.at[place2, hist]
+    gy4 = along_hist(own4, own4, gy4_sem)
 
     finish(x2)
     total = sum2[x]
@@ -537,6 +546,9 @@
     finish(gx1)
     line1 = gathered1.at[hist, pl.ds(mine + z * XS, XS)]
     gz1 = along_z(lambda there: line1, line1, gz1_sem)
+    finish(gy4)
+    all4 = gathered4.at[place2]
+    gz4 = along_z(lambda there: all4, all4, gz4_sem)
 
     finish(z2)
     shard2 = z_send2[z]
@@ -552,9 +564,12 @@
     plane1 = gathered1.at[hist, half]
     last = [to_core(plane1, plane1, gc1_sem, 0)]
     gy1 = along_hist(plane1, plane1, gy1_sem)
+    finish(gz4)
+    line4 = gathered4.at[pl.ds(mine + x * ZS, ZS)]
+    gx4 = along_x(lambda there: line4, line4, gx4_sem)
+    last.append(to_core(line4, line4, gc4_sem, 0))
 
     finish(y2)
-    place2 = mine + x * ZS + z
     for b in range(2):
         wide = jnp.concatenate([y_recv2[2 * b, :8, :], y_recv2[2 * b + 1, :8, :]], axis=1)
         high = wide.astype(bf16).astype(f32)
@@ -582,6 +597,10 @@
         came = gathered1.at[lax.rem(hist + HIST - i, HIST), half]
         last.append(to_core(came, came, gc1_sem, i))
     for i in range(1, XS):
+        gx4[i - 1].wait()
+        came = gathered4.at[pl.ds(mine + lax.rem(x + XS - i, XS) * ZS, ZS)]
+        last.append(to_core(came, came, gc4_sem, i))
+    for i in range(1, XS):
         gx2[i - 1].wait()
         came = gathered2.at[pl.ds(mine + lax.rem(x + XS - i, XS) * ZS, ZS)]
         last.append(to_core(came, came, gc2_sem, i))
@@ -610,6 +629,7 @@
     gathered1_in,
     gathered2_in,
     gathered3_in,
+    gathered4_in,
     result_in,
     out_states,
     out_neigh,
@@ -620,6 +640,7 @@
     gathered1,
     gathered2,
     gathered3,
+    gathered4,
     result,
     new_states,
     new_neigh,
@@ -636,6 +657,7 @@
         (result_in, result),
         (gathered2_in, gathered2),
         (gathered3_in, gathered3),
+        (gathered4_in, gathered4),
     ):
         fetched.append(pltpu.make_async_copy(src, dst, in_sem.at[len(fetched)]))
         fetched[-1].start()
@@ -646,11 +668,10 @@
         stored[-1].start()
 
     fetched[0].wait()
-    for at, new, out in ((R_GATE, new_gate, out_gate), (R_SELF, new_self, out_self)):
-        for h in range(HIST):
-            rows = gathered1[h].astype(f32)[:, at : at + 8, :] * factor
-            new[:, h * QUART : (h + 1) * QUART] = rows.reshape(D, QUART)
-        store(new, out)
+    for h in range(HIST):
+        rows = gathered1[h].astype(f32) * factor
+        new_gate[:, h * QUART : (h + 1) * QUART] = rows.reshape(D, QUART)
+    store(new_gate, out_gate)
     fetched[1].wait()
     for h in range(HIST):
         new_states[0, :, h * QUART : (h + 1) * QUART] = result[h].astype(f32)
@@ -670,6 +691,13 @@
             at = g % ZS * XS + g // ZS
             new_neigh[h // 2, g * 8 : (g + 1) * 8, lanes] = rows[at]
     store(new_neigh, out_neigh)
+    fetched[4].wait()
+    for h in range(HIST):
+        rows = gathered4[:, h].astype(f32) * factor
+        for g in range(ENT):
+            at = g // GROUP * GROUP + g % XS * ZS + g % GROUP // XS
+            new_self[g * 8 : (g + 1) * 8, h * QUART : (h + 1) * QUART] = rows[at]
+    store(new_self, out_self)
     store(new_bias, out_bias)
     for copy in stored:
         copy.wait()
@@ -697,16 +725,17 @@
     shape = jax.ShapeDtypeStruct
     v = pltpu.VMEM
     i32 = jnp.int32
-    gathered1, gathered2, gathered3, result = pl.pallas_call(
+    gathered1, gathered2, gathered3, gathered4, result = pl.pallas_call(
         kernel,
         out_shape=(
             shape((HIST, ENT, KEPT, QUART), bf16),
             shape((ENT, HIST, 8, QUART), bf16),
             shape((HIST, ENT, 8, QUART), bf16),
+            shape((ENT, HIST, 8, QUART), bf16),
             shape((HIST, ROWS, QUART), bf16),
         ),
         in_specs=[anywhere] * 13,
-        out_specs=(vmem,) * 4,
+        out_specs=(vmem,) * 5,
         scratch_shapes=[
             v((HIST, 2, ROWS, HALF), bf16),
             v((HALF, QUART), bf16),
@@ -788,6 +817,10 @@
             dma((2, ZS)),
             dma((2, HIST)),
             dma((2, HIST)),
+            dma((2, HIST)),
+            dma((2, ZS)),
+            dma((2, XS)),
+            dma((2, XS)),
         ],
         compiler_params=pltpu.CompilerParams(
             collective_id=0, has_side_effects=True, vmem_limit_bytes=54 << 20
@@ -818,12 +851,13 @@
             shape((1, D), f32),
             shape((NREL, D), f32),
         ),
-        in_specs=[anywhere] * 4,
+        in_specs=[anywhere] * 5,
         out_specs=(anywhere,) * 6,
         scratch_shapes=[
             v((HIST, ENT, KEPT, QUART), bf16),
             v((ENT, HIST, 8, QUART), bf16),
             v((HIST, ENT, 8, QUART), bf16),
+            v((ENT, HIST, 8, QUART), bf16),
             v((HIST, ROWS, QUART), bf16),
             v((1, ROWS, D), f32),
             v((2, HALF, HALF), f32),
@@ -831,12 +865,12 @@
             v((D, D), f32),
             v((1, D), f32),
             v((NREL, D), f32),
-            dma((4,)),
+            dma((5,)),
             dma((6,)),
         ],
         compiler_params=pltpu.CompilerParams(vmem_limit_bytes=54 << 20),
         name="unfold",
-    )(gathered1, gathered2, gathered3, result)
+    )(gathered1, gathered2, gathered3, gathered4, result)
     return result, grad_neigh, grad_self, grad_gate, grad_bias.reshape(D), grad_rel
 
 

time: 107 us -> 108 us (level)
  no operation moved by 1% of the time
where the time goes in v6:
time: 108 us; the launch traced here: 107 us
  Pallas kernels  107 us (99%)
    pallas_call x1, Pallas kernels, on_device(): pl.pallas_call(kernel, out_shape=(shape((HIST, ENT, KEPT, QUART), bf16),...  104 us
    pallas_call x1, Pallas kernels, on_device(): pl.pallas_call(functools.partial(unfold, factor), out_shape=(shape((1, RO...  3.25 us

profile of v6, /device:TPU:1, one launch (start us, length us, event | category | flops | bytes accessed | tf_op | source)
XLA Modules:
  0.0 107.4 jit_solution(17268619679062237742)
XLA Ops:
  0.6 103.6 %encoder_backward.1 = (bf16[4,64,8,128]{3,2,1,0:T(8,128)(2,1)}, bf16[64,4,8,128]{3,2,1,0:T(8,128)(2,1)}, bf16[4,64,8,128]{3,2,1,0:T(8,128)(2,1)}, bf16[64,4,8,128]{3,2,1,0:T(8,128)(2,1)}, bf16[4,256,128]{2,1,0:T(8,128)(2,1)}) custom-call(bf16[1,256,512]{2,1,0:T(8,128)(2,1)} %states_in.1, bf16[2,256,256]{2,1,0:T(8,128)(2,1)} %w_neigh_in.1, ...), custom_call_target="tpu_custom_call" | custom-call | tf_op jit(solution)/shard_map/encoder_backward/pallas_call | solution.py:728
  104.2 3.2 %unfold.1 = (f32[1,256,512]{2,1,0:T(8,128)}, f32[2,256,256]{2,1,0:T(8,128)}, f32[512,512]{1,0:T(8,128)}, f32[512,512]{1,0:T(8,128)}, f32[1,512]{1,0:T(1,128)}, /*index=5*/f32[460,512]{1,0:T(8,128)}) custom-call(bf16[4,64,8,128]{3,2,1,0:T(8,128)(2,1)} %get-tuple-element.17.gathered1_in, bf16[64,4,8,128]{3,2,1,0:T(8,128)(2,1)} %get-tuple-element.18.gathered2_in, ...), custom_call_target="tpu_custom_call" | custom-call | tf_op jit(solution)/shard_map/unfold/pallas_call | solution.py:844
